TPU v7x, 32 devices: a whole 2x2x4 slice. The times are simulated.
32 devices in a mesh: gz: 8 (over y, x, core), gy: 4 (over z).
Axes of the slice: x: 2, y: 2, z: 4, core: 2. Of those that a mesh axis runs over, the one named last changes fastest.
Arguments:
- coarse_six: float32 [64, 1024, 512], P('gz', 'gy'), may hold values from 0.1 to 10
Outputs:
- detail_seven: float32 [64, 1024, 512], P('gz', 'gy')
- coarse_seven: float32 [64, 1024, 512], P('gz', 'gy')
All inputs are finite; a program needn't handle non-finite values.
Results may differ from a plain program's by a relative error of at most 0.00002.
Values sent between devices are 32-bit elements; how exact they have to be, the bound alone decides.
No kernel may reach another device: no remote copies, remote signals or barrier semaphores. Data moves between devices by JAX's collectives and lax.ppermute only.
A program may use at most 128 MiB of HBM per device.

v0:
```python
import functools
import math

import jax
import jax.numpy as jnp
from jax import lax
from jax.experimental import pallas as pl
from jax.experimental.pallas import tpu as pltpu
from jax.sharding import PartitionSpec as P

TAP_DILATION = 32
REACH = 2 * TAP_DILATION
LANES = 128
STRIP = 8
UNIT_ROWS = 128
FIRST_PLANES = 2
LEAD_UNITS = 2
LATER_GROUPS = (((2, 0),), ((2, 0),), ((1, 1), (1, 2)))
SHORT_FIRST = 2

kernel_weights = (0.0625, 0.25, 0.375, 0.25, 0.0625)


def passed_along(x, axis, by):
    peers = lax.axis_size(axis)
    return lax.ppermute(x, axis, [(i, (i + by) % peers) for i in range(peers)])


def z_taps(plane_stack, count):
    weights = {}
    for cell_position in range(5):
        filter_reach = (cell_position - 2) * TAP_DILATION // plane_stack
        moved = -filter_reach % count
        weights[moved] = weights.get(moved, 0.0) + kernel_weights[cell_position]
    own = weights.pop(0, 0.0)
    return own, weights


def lane_of(shape):
    return lax.broadcasted_iota(jnp.int32, shape, 1)


def x_taps():
    return {(cell_position - 2) * TAP_DILATION: kernel_weights[cell_position] for cell_position in range(5)}


def rest_taps():
    return {(cell_position - 2) * TAP_DILATION: weight for cell_position, weight in enumerate((0.125, 0.375, 0.375, 0.125))}


def pair_sums(rows):
    return (rows + pltpu.roll(rows, rows.shape[1] - TAP_DILATION, 1)) * 0.5


def fill_matrix(matrix_ref, taps):
    depth, width = matrix_ref.shape
    for start in range(0, depth, LANES):
        shape = (LANES, width)
        row = start + lax.broadcasted_iota(jnp.int32, shape, 0)
        offset = row - lax.broadcasted_iota(jnp.int32, shape, 1)
        offset = jnp.where(offset < 0, offset + width, offset)
        values = jnp.zeros(shape, jnp.float32)
        for tap, weight in taps.items():
            values = jnp.where(offset == tap % width, weight, values)
        matrix_ref[pl.ds(start, LANES), :] = values.astype(jnp.bfloat16)


def x_smoothed(rows, matrix):
    parts = []
    for _ in range(3):
        parts.append(rows.astype(jnp.bfloat16))
        rows = rows - parts[-1].astype(jnp.float32)
    terms = jnp.dot(jnp.concatenate(parts), matrix, preferred_element_type=jnp.float32)
    high, middle, low = jnp.split(terms, 3)
    return high + middle + low


def y_sums(groups):
    for _ in range(4):
        groups = [a + b for a, b in zip(groups[:-1], groups[1:])]
    return groups


def packed_rows(width):
    return UNIT_ROWS - UNIT_ROWS * TAP_DILATION // width


def store_packed(out_ref, place, smooth):
    rows, width = smooth.shape
    kept_rows = out_ref.shape[1]
    depth = rows - kept_rows
    out_ref[place, :, : width - LANES] = smooth[:kept_rows, : width - LANES]
    kept = lane_of((depth, LANES)) < LANES - TAP_DILATION
    for piece in range(kept_rows // depth):
        tile = piece * TAP_DILATION // LANES
        shift = (LANES - TAP_DILATION - piece * TAP_DILATION) % LANES
        moved = smooth[kept_rows:, tile * LANES : (tile + 1) * LANES]
        if shift:
            moved = pltpu.roll(moved, shift, 1)
        last = smooth[piece * depth : (piece + 1) * depth, width - LANES :]
        out_ref[place, pl.ds(piece * depth, depth), width - LANES :] = jnp.where(kept, last, moved)


def completed(strip):
    width = strip.shape[1]
    last = strip[:, width - LANES :]
    lane = lane_of(last.shape)
    kept = lane < LANES - TAP_DILATION
    total = jnp.where(kept, last, 0.0)
    for start in range(0, width - LANES, LANES):
        total = total + strip[:, start : start + LANES]
    odd = (lane // TAP_DILATION) % 2 == 1
    total = jnp.where(odd, -total, total)
    total = total + pltpu.roll(total, 2 * TAP_DILATION, 1)
    total = total + pltpu.roll(total, TAP_DILATION, 1)
    return jnp.concatenate([strip[:, : width - LANES], jnp.where(kept, last, total)], axis=1)


def unpacked(weights, refs, use):
    kept_rows, width = refs[0].shape[1:]
    depth = UNIT_ROWS - kept_rows
    tiles = [None] * (width // LANES)
    for piece in range(kept_rows // depth):
        rows = pl.ds(piece * depth, depth)
        strip = weighted(weights, [ref[0, rows, :] for ref in refs])
        tile = piece * TAP_DILATION // LANES
        shift = (piece * TAP_DILATION - (LANES - TAP_DILATION)) % LANES
        moved = strip[:, width - LANES :]
        if shift:
            moved = pltpu.roll(moved, shift, 1)
        if tiles[tile] is None:
            tiles[tile] = moved
        else:
            here = lane_of(moved.shape) // TAP_DILATION == piece % (LANES // TAP_DILATION)
            tiles[tile] = jnp.where(here, moved, tiles[tile])
        use(rows, completed(strip))
    use(pl.ds(kept_rows, depth), completed(jnp.concatenate(tiles, axis=1)))


def weighted(weights, values):
    total = None
    for weight, value in zip(weights, values):
        term = weight * value
        total = term if total is None else total + term
    return total


def pair_kernel(units_ref, out_ref, read_ref, read_sems):
    def read(unit):
        return pltpu.make_async_copy(units_ref.at[unit], read_ref.at[unit], read_sems.at[unit])

    for unit in range(out_ref.shape[0]):
        read(unit).start()
    for unit in range(out_ref.shape[0]):
        read(unit).wait()
        store_packed(out_ref, unit, pair_sums(read_ref[unit]))


def x_kernel(first, units_ref, out_ref, read_ref, matrix_ref, read_sems):
    count = out_ref.shape[0]

    def read(unit):
        return pltpu.make_async_copy(units_ref.at[first + unit], read_ref.at[unit], read_sems.at[unit])

    for unit in range(count):
        read(unit).start()
    fill_matrix(matrix_ref, x_taps())

    @pl.loop(0, count)
    def _(unit):
        read(unit).wait()
        store_packed(out_ref, unit, x_smoothed(read_ref[unit], matrix_ref[...]))


def extended_groups(before_ref, c_ref, after_ref, offset):
    groups = []
    for ref in (before_ref, c_ref, after_ref):
        for start in range(0, ref.shape[1], TAP_DILATION):
            groups.append(ref[0, pl.ds(start + offset, STRIP), :])
    return groups


def y_smoothed(before_ref, c_ref, after_ref, smooth_ref):
    for within in range(TAP_DILATION // STRIP):
        groups = y_sums(extended_groups(before_ref, c_ref, after_ref, within * STRIP))
        for group, strip in enumerate(groups):
            smooth_ref[pl.ds(group * TAP_DILATION + within * STRIP, STRIP), :] = strip * (1.0 / 16.0)


def yx_kernel(before_ref, c_ref, after_ref, *refs):
    *out_refs, matrix_ref, smooth_ref = refs
    pl.when(pl.program_id(0) == 0)(lambda: fill_matrix(matrix_ref, x_taps()))
    y_smoothed(before_ref, c_ref, after_ref, smooth_ref)
    places = [(ref, place) for ref in out_refs for place in range(ref.shape[0])]
    for unit, (ref, place) in enumerate(places):
        smooth = x_smoothed(smooth_ref[pl.ds(unit * UNIT_ROWS, UNIT_ROWS), :], matrix_ref[...])
        store_packed(ref, place, smooth)


def z_kernel(weights, *refs):
    whole_ref = refs[-1]

    def use(rows, strip):
        whole_ref[0, rows, :] = strip

    unpacked(weights, refs[: len(weights)], use)


def group_of(shape):
    return lane_of(shape) // TAP_DILATION


def spread(tile, group):
    tile = jnp.where(group_of(tile.shape) == group, tile, 0.0)
    tile = tile + pltpu.roll(tile, 2 * TAP_DILATION, 1)
    return tile + pltpu.roll(tile, TAP_DILATION, 1)


def strip_rows(rows, ahead):
    per_group = TAP_DILATION // STRIP
    strip = lax.rem(lax.axis_index("gy") + ahead, per_group)
    return pl.ds(pl.multiple_of(rows - TAP_DILATION + strip * STRIP, STRIP), STRIP)


def short_strips(rows):
    half = rows - UNIT_ROWS
    fixed = [pl.ds(row, STRIP) for row in range(0, rows - TAP_DILATION, STRIP)]
    moving = [strip_rows(rows, ahead) for ahead in range(1, TAP_DILATION // STRIP)]
    return fixed[: half // STRIP], fixed[half // STRIP :] + moving


def short_tiles(rows, width):
    return (rows // STRIP - 3) * (width // LANES)


def short_kernel(before_ref, c_ref, after_ref, out_ref, matrix_ref, smooth_ref):
    plane = pl.program_id(0)

    @pl.when(plane == 0)
    def _():
        fill_matrix(matrix_ref, x_taps())
        out_ref[out_ref.shape[0] - 1] = jnp.zeros((STRIP, LANES), jnp.float32)

    y_smoothed(before_ref, c_ref, after_ref, smooth_ref)
    rows, width = smooth_ref.shape
    for start in range(0, rows, UNIT_ROWS):
        unit = pl.ds(start, UNIT_ROWS)
        smooth_ref[unit, :] = x_smoothed(smooth_ref[unit, :], matrix_ref[...])
    index = plane * short_tiles(rows, width)
    groups = LANES // TAP_DILATION
    for places in short_strips(rows):
        *places, last_place = places
        last = smooth_ref[last_place, :]
        for piece, place in enumerate(places):
            strip = smooth_ref[place, :]
            tile = piece // groups * LANES
            moved = last[:, tile : tile + LANES]
            shift = (groups - 1 - piece) % groups * TAP_DILATION
            if shift:
                moved = pltpu.roll(moved, shift, 1)
            for start in range(0, width - LANES, LANES):
                out_ref[index] = strip[:, start : start + LANES]
                index += 1
            here = group_of(moved.shape) == groups - 1
            out_ref[index] = jnp.where(here, moved, strip[:, width - LANES :])
            index += 1
    left = spread(last[:, width - LANES :], groups - 2)
    end = out_ref.shape[0] - 1
    out_ref[end] = jnp.where(group_of(left.shape) == plane, left, out_ref[end])


def short_z_kernel(weights, *refs):
    packed, (whole_ref, *sum_refs) = refs[: len(weights)], refs[-4:]
    rows, width = whole_ref.shape[1:]
    plane = pl.program_id(0)
    index = plane * short_tiles(rows, width)
    groups, tiles = LANES // TAP_DILATION, width // LANES
    for places in short_strips(rows):
        *places, last_place = places
        last = [None] * tiles
        for piece, place in enumerate(places):
            strip = [weighted(weights, [ref[index + tile] for ref in packed]) for tile in range(tiles)]
            index += tiles
            tile, group = divmod(piece, groups)
            shift = (group + 1 - groups) % groups * TAP_DILATION
            moved = pltpu.roll(strip[-1], shift, 1) if shift else strip[-1]
            here = group_of(moved.shape) == group
            last[tile] = moved if last[tile] is None else jnp.where(here, moved, last[tile])
            whole_ref[0, place, :] = completed(jnp.concatenate(strip, axis=1))
        if len(places) < tiles * groups - 1:
            end = packed[0].shape[0] - 1
            left = spread(weighted(weights, [ref[end] for ref in packed]), plane)
            last[-1] = jnp.where(group_of(left.shape) == groups - 2, left, last[-1])
        whole_ref[0, last_place, :] = completed(jnp.concatenate(last, axis=1))

    groups = rows // TAP_DILATION
    for ahead in range(TAP_DILATION // STRIP):
        total = None
        for group in range(groups if ahead else groups - 1):
            strip = whole_ref[0, strip_rows((group + 1) * TAP_DILATION, ahead), :]
            if total is None:
                total = strip
            else:
                total = total + strip if group % 2 == 0 else total - strip
        if ahead:
            sum_refs[ahead - 1][0] = total
        else:
            whole_ref[0, strip_rows(rows, 0), :] = total


def short_finish_kernel(whole_ref, *refs):
    *sum_refs, c_ref, _, _, detail_ref, coarse_ref = refs
    missing = strip_rows(whole_ref.shape[1], 0)
    coarse_ref[...] = whole_ref[...]
    coarse_ref[0, missing, :] = whole_ref[0, missing, :] + sum(ref[0] for ref in sum_refs)
    detail_ref[...] = c_ref[...] - coarse_ref[...]


def pair_z_kernel(weights, *refs):
    whole_ref, matrix_ref, pair_ref = refs[-3:]
    pl.when(pl.program_id(0) == 0)(lambda: fill_matrix(matrix_ref, rest_taps()))

    def use(rows, strip):
        pair_ref[rows, :] = strip

    unpacked(weights, refs[: len(weights)], use)
    whole_ref[0] = x_smoothed(pair_ref[...], matrix_ref[...])


def y_kernel(before_ref, whole_ref, after_ref, c_ref, detail_ref, coarse_ref):
    scale = 1.0 / 16.0
    for within in range(TAP_DILATION // STRIP):
        groups = y_sums(extended_groups(before_ref, whole_ref, after_ref, within * STRIP))
        for group, strip in enumerate(groups):
            rows = pl.ds(group * TAP_DILATION + within * STRIP, STRIP)
            coarse = strip * scale
            coarse_ref[0, rows, :] = coarse
            detail_ref[0, rows, :] = c_ref[0, rows, :] - coarse


def finish_kernel(weights, *refs):
    c_ref, _, _, detail_ref, coarse_ref = refs[len(weights) :]

    def use(rows, strip):
        coarse_ref[0, rows, :] = strip
        detail_ref[0, rows, :] = c_ref[0, rows, :] - strip

    unpacked(weights, refs[: len(weights)], use)


def last_kernel(weights, place, *refs):
    units_ref, _, _, detail_ref, coarse_ref, results_ref, write_sems = refs[len(weights) :]
    half = UNIT_ROWS // 2

    def write(piece, output, ref):
        rows = pl.ds(piece * half, half)
        source = results_ref.at[output, rows]
        return pltpu.make_async_copy(source, ref.at[place, rows], write_sems.at[piece, output])

    writes = [[write(piece, 0, detail_ref), write(piece, 1, coarse_ref)] for piece in range(2)]

    def use(rows, strip):
        results_ref[1, rows, :] = strip
        results_ref[0, rows, :] = units_ref[place, rows, :] - strip
        piece, left = divmod(rows.start + rows.size, half)
        if left == 0:
            for copy in writes[piece - 1]:
                copy.start()

    unpacked(weights, refs[: len(weights)], use)
    for copies in writes:
        for copy in copies:
            copy.wait()


def block_of(rows, width, first=0, depth=1):
    return pl.BlockSpec((depth, rows, width), lambda step: (first + step, 0, 0))


def anywhere():
    return pl.BlockSpec(memory_space=pl.ANY)


def tiles_of(pieces):
    return pl.BlockSpec((pieces, STRIP, LANES), lambda step: (0, 0, 0))


def in_vmem():
    return pl.BlockSpec(memory_space=pltpu.VMEM)


def call(kernel, name, steps, in_specs, out_specs, out_shape, args, aliases=None, scratch=(), grant=24):
    blocks = [spec.block_shape for spec in (*in_specs, *out_specs) if spec.block_shape]
    moved = 4 * max(steps, 1) * sum(math.prod(block) for block in blocks)
    return pl.pallas_call(
        kernel,
        grid=(steps,) if steps else (),
        in_specs=in_specs,
        out_specs=out_specs,
        out_shape=out_shape,
        scratch_shapes=scratch,
        input_output_aliases=aliases or {},
        compiler_params=pltpu.CompilerParams(vmem_limit_bytes=grant * 1024 * 1024),
        cost_estimate=pl.CostEstimate(flops=moved * 2, bytes_accessed=moved, transcendentals=0),
        name=name,
    )(*args)


def in_hbm(x):
    return pltpu.with_memory_space_constraint(x, pltpu.HBM)


def f32(*shape):
    return jax.ShapeDtypeStruct(shape, jnp.float32)


def can_shorten(rows, width):
    strips = TAP_DILATION // STRIP
    return lax.axis_size("gy") == strips and rows // TAP_DILATION % 2 == 0 and UNIT_ROWS // STRIP == width // TAP_DILATION


def shards(coarse_six):
    planes, rows, width = coarse_six.shape
    short = packed_rows(width)
    own, shifts = z_taps(planes, lax.axis_size("gz"))
    weights = (own, *shifts.values())
    count = len(weights)
    whole, unit, packed, edge = (functools.partial(block_of, n, width) for n in (rows, UNIT_ROWS, short, REACH))
    parts = rows // UNIT_ROWS
    units = coarse_six.reshape(planes * parts, UNIT_ROWS, width)
    matrix = pltpu.VMEM((width, width), jnp.bfloat16)

    def along_gz(x):
        return [passed_along(x, "gz", moved) for moved in shifts]

    def halo(source, start, stop):
        top, bottom = source[start:stop, :REACH], source[start:stop, rows - REACH :]
        return passed_along(bottom, "gy", 1), passed_along(top, "gy", -1)

    sums_shape = f32(FIRST_PLANES * parts, UNIT_ROWS, width)
    lead = call(
        pair_kernel,
        "pair_x",
        0,
        [anywhere()],
        [in_vmem()],
        [pltpu.VMEM((LEAD_UNITS, short, width), jnp.float32)],
        [in_hbm(units)],
        scratch=[pltpu.VMEM((LEAD_UNITS, UNIT_ROWS, width), jnp.float32), pltpu.SemaphoreType.DMA((LEAD_UNITS,))],
    )[0]
    lead, ready = lax.optimization_barrier((lead, units))
    lead_moved = along_gz(lead)
    first = FIRST_PLANES * parts - LEAD_UNITS
    first_block = call(
        functools.partial(x_kernel, LEAD_UNITS),
        "smooth_x",
        0,
        [anywhere()],
        [in_vmem()],
        [pltpu.VMEM((first, short, width), jnp.float32)],
        [in_hbm(ready)],
        scratch=[
            pltpu.VMEM((first, UNIT_ROWS, width), jnp.float32),
            matrix,
            pltpu.SemaphoreType.DMA((first,)),
        ],
    )[0]
    first_block, ready = lax.optimization_barrier((first_block, coarse_six))
    first_moved = along_gz(first_block)
    sums = call(
        functools.partial(pair_z_kernel, weights),
        "smooth_zx",
        LEAD_UNITS,
        [packed()] * count,
        [unit()],
        [sums_shape],
        [lead, *lead_moved],
        scratch=[matrix, pltpu.VMEM((UNIT_ROWS, width), jnp.float32)],
    )

    later, short_sent = [], []
    start = FIRST_PLANES
    near = halo(ready, start, start + sum(size for size, _ in LATER_GROUPS[0]))
    near, sums = lax.optimization_barrier((near, sums))
    for number, sizes in enumerate(LATER_GROUPS):
        offset = 0
        for size, messages in sizes:
            place = start + offset
            sources = [near[0], in_hbm(coarse_six), near[1]]
            specs = [edge(offset), whole(place), edge(offset)]
            scratch = [matrix, pltpu.VMEM((rows, width), jnp.float32)]
            if messages or not can_shorten(rows, width):
                messages = max(messages, 1)
                depth = parts // messages
                blocks = call(
                    yx_kernel,
                    "smooth_yx",
                    size,
                    specs,
                    [packed(depth=depth)] * messages,
                    [f32(size * depth, short, width)] * messages,
                    sources,
                    scratch=scratch,
                )
                for message, block in enumerate(blocks):
                    later.append((place * parts + message * depth, size * depth, (block, *along_gz(block))))
            else:
                pieces = size * short_tiles(rows, width) + 1
                block = call(
                    short_kernel,
                    "smooth_yx_short",
                    size,
                    specs,
                    [tiles_of(pieces)],
                    [f32(pieces, STRIP, LANES)],
                    sources,
                    scratch=scratch,
                )[0]
                short_sent.append((place, size, (block, *along_gz(block))))
            offset += size
        start += offset
        if number == 0:
            block, ready = lax.optimization_barrier((block, ready))
            block, *first_moved = lax.optimization_barrier((block, *first_moved))
            sums = call(
                functools.partial(z_kernel, weights),
                "smooth_z",
                first,
                [packed()] * count + [anywhere()],
                [unit(LEAD_UNITS)],
                [sums_shape],
                [first_block, *first_moved, *sums],
                {count: 0},
            )[0]
            along_z = sums.reshape(FIRST_PLANES, rows, width)
        if number + 1 < len(LATER_GROUPS):
            block, ready = lax.optimization_barrier((block, ready))
            near = halo(ready, start, start + sum(size for size, _ in LATER_GROUPS[number + 1]))
        if number and short_sent:
            near, _ = lax.optimization_barrier((near, short_sent[0][2]))
        if number == 0:
            near, along_z = lax.optimization_barrier((near, along_z))
            sides = halo(along_z, 0, FIRST_PLANES)

    def sum_short(batch):
        planes_in = sum(size for _, size, _ in batch)
        step, sums = 0, []
        for _, size, blocks in batch:
            sums = call(
                functools.partial(short_z_kernel, weights),
                "smooth_z_short",
                size,
                [tiles_of(blocks[0].shape[0])] * count + [anywhere()] * len(sums),
                [whole(step)] + [block_of(STRIP, width, step)] * 3,
                [f32(planes_in, rows, width)] + [f32(planes_in, STRIP, width)] * 3,
                [*blocks, *sums],
                {count + at: at for at in range(len(sums))},
            )
            step += size
        return sums[0], [passed_along(total, "gy", ahead) for ahead, total in enumerate(sums[1:], 1)]

    def finish_short(batch, sums, outs):
        start, size = batch[0][0], sum(size for _, size, _ in batch)
        along_z, moved = sums
        outs, moved = lax.optimization_barrier((outs, moved))
        return call(
            short_finish_kernel,
            "finish_short",
            size,
            [whole()] + [block_of(STRIP, width)] * 3 + [whole(start)] + [anywhere()] * 2,
            [whole(start)] * 2,
            [f32(planes, rows, width)] * 2,
            [along_z, *moved, coarse_six, *outs],
            {5: 0, 6: 1},
        )

    batches = [batch for batch in (short_sent[:SHORT_FIRST], short_sent[SHORT_FIRST:]) if batch]
    block, sides = lax.optimization_barrier((block, sides))
    outs = call(
        y_kernel,
        "smooth_y",
        FIRST_PLANES,
        [edge(), whole(), edge(), whole()],
        [whole(), whole()],
        [f32(planes, rows, width)] * 2,
        [sides[0], along_z, sides[1], coarse_six],
    )
    for batch in batches:
        outs, blocks = lax.optimization_barrier((outs, [blocks for _, _, blocks in batch]))
        sums = sum_short([(place, size, block) for (place, size, _), block in zip(batch, blocks)])
        outs = finish_short(batch, sums, outs)
    outs = [out.reshape(units.shape) for out in outs]
    for place, size, blocks in later[:-1]:
        outs, blocks = lax.optimization_barrier((outs, blocks))
        outs = call(
            functools.partial(finish_kernel, weights),
            "finish",
            size,
            [packed()] * count + [unit(place)] + [anywhere()] * 2,
            [unit(place)] * 2,
            [f32(*units.shape)] * 2,
            [*blocks, units, *outs],
            {count + 1: 0, count + 2: 1},
        )
    place, _, blocks = later[-1]
    outs, blocks = lax.optimization_barrier((outs, blocks))
    outs = call(
        functools.partial(last_kernel, weights, place),
        "finish_last",
        0,
        [in_vmem()] * (count + 1) + [anywhere()] * 2,
        [anywhere()] * 2,
        [f32(*units.shape)] * 2,
        [*blocks, units, *outs],
        {count + 1: 0, count + 2: 1},
        scratch=[
            pltpu.VMEM((2, UNIT_ROWS, width), jnp.float32),
            pltpu.SemaphoreType.DMA((2, 2)),
        ],
    )
    return tuple(out.reshape(coarse_six.shape) for out in outs)


def solution(mesh):
    return jax.shard_map(
        shards,
        mesh=mesh,
        in_specs=(P("gz", "gy", None),),
        out_specs=(P("gz", "gy", None), P("gz", "gy", None)),
        check_vma=False,
    )
```

profile of v0, /device:TPU:0, one launch (start us, length us, event | category | flops | bytes accessed | tf_op | source)
XLA Modules:
  0.0 92.2 jit_solution(17059253322006313305)
XLA Ops:
  0.6 1.3 %pair_x.1.refs_0_ = f32[2,120,512]{2,1,0:T(8,128)S(1)} custom-call(f32[16,128,512]{2,1,0:T(8,128)} %bitcast.6), custom_call_target="tpu_custom_call" | custom-call | tf_op jit(solution)/shard_map/pair_x/pallas_call | solution.py:395
  1.9 3.0 %collective-permute-start.2 = (f32[2,120,512]{2,1,0:T(8,128)S(1)}, f32[2,120,512]{2,1,0:T(8,128)S(1)}, u32[]{:S(2)}, u32[]{:S(2)}) collective-permute-start(f32[2,120,512]{2,1,0:T(8,128)S(1)} %pair_x.1.refs_0_), channel_id=1, source_target_pairs={{0,16},{4,20},{8,24},{12,28},{16,0},{20,4},{24,8},{28,12},{1,17},{... | collective-permute-start | bytes 1474568 | tf_op jit(solution)/shard_map/ppermute | solution.py:26
  5.0 1.9 %smooth_x.1.refs_0_ = f32[2,120,512]{2,1,0:T(8,128)S(1)} custom-call(f32[16,128,512]{2,1,0:T(8,128)} %bitcast.7), custom_call_target="tpu_custom_call" | custom-call | tf_op jit(solution)/shard_map/smooth_x/pallas_call | solution.py:395
  6.9 1.1 %fusion.2 = (f32[2,64,512]{2,1,0:T(8,128)S(1)}, f32[2,64,512]{2,1,0:T(8,128)S(1)}) fusion(f32[8,256,512]{2,1,0:T(8,128)} %c_ref.9), kind=kLoop, calls=%fused_computation.2 | loop fusion | bytes 1048576 | tf_op jit(solution)/shard_map/slice | solution.py:437
  7.9 1.6 %collective-permute-start = (f32[2,64,512]{2,1,0:T(8,128)S(1)}, f32[2,64,512]{2,1,0:T(8,128)S(1)}, u32[]{:S(2)}, u32[]{:S(2)}) collective-permute-start(f32[2,64,512]{2,1,0:T(8,128)S(1)} %get-tuple-element.125), channel_id=1, source_target_pairs={{0,1},{1,2},{2,3},{3,0},{4,5},{5,6},{6,7},{7,4},{8,9},{9,10},{10,1... | collective-permute-start | bytes 786440 | tf_op jit(solution)/shard_map/ppermute | solution.py:26
  9.6 2.2 %collective-permute-start.1 = (f32[2,64,512]{2,1,0:T(8,128)S(1)}, f32[2,64,512]{2,1,0:T(8,128)S(1)}, u32[]{:S(2)}, u32[]{:S(2)}) collective-permute-start(f32[2,64,512]{2,1,0:T(8,128)S(1)} %get-tuple-element.124), channel_id=1, source_target_pairs={{0,3},{1,0},{2,1},{3,2},{4,7},{5,4},{6,5},{7,6},{8,11},{9,8},{10,9... | collective-permute-start | bytes 786440 | tf_op jit(solution)/shard_map/ppermute | solution.py:26
  11.8 0.3 collective-permute-start.5
  12.1 4.9 %collective-permute-done.2.refs_1_ = f32[2,120,512]{2,1,0:T(8,128)S(1)} collective-permute-done((f32[2,120,512]{2,1,0:T(8,128)S(1)}, f32[2,120,512]{2,1,0:T(8,128)S(1)}, u32[]{:S(2)}, u32[]{:S(2)}) %collective-permute-start.2) | collective-permute-done | bytes 491552 | tf_op jit(solution)/shard_map/ppermute | solution.py:26
  17.0 1.1 %smooth_zx.1.refs_2_ = f32[4,128,512]{2,1,0:T(8,128)S(1)} custom-call(f32[2,120,512]{2,1,0:T(8,128)S(1)} %pair_x.1.refs_0_, f32[2,120,512]{2,1,0:T(8,128)S(1)} %collective-permute-done.2.refs_1_), custom_call_target="tpu_custom_call" | custom-call | flops 3014656 | bytes 1507328 | tf_op jit(solution)/shard_map/smooth_zx/pallas_call | solution.py:395
  18.1 0.9 collective-permute-done.before_ref
  19.0 3.6 %collective-permute-done.1.after_ref = f32[2,64,512]{2,1,0:T(8,128)S(1)} collective-permute-done((f32[2,64,512]{2,1,0:T(8,128)S(1)}, f32[2,64,512]{2,1,0:T(8,128)S(1)}, u32[]{:S(2)}, u32[]{:S(2)}) %collective-permute-start.1) | collective-permute-done | bytes 262176 | tf_op jit(solution)/shard_map/ppermute | solution.py:26
  22.7 2.7 %smooth_yx_short.2.refs_0_ = f32[233,8,128]{2,1,0:T(8,128)S(1)} custom-call(f32[2,64,512]{2,1,0:T(8,128)S(1)} %collective-permute-done.before_ref, f32[8,256,512]{2,1,0:T(8,128)} %c_ref.9, f32[2,64,512]{2,1,0:T(8,128)S(1)} %collective-permute-done.1.after_ref), custom_call_target="tpu_custom_call" | custom-call | flops 6963200 | bytes 3481600 | tf_op jit(solution)/shard_map/smooth_yx_short/pallas_call | solution.py:395
  25.4 0.6 collective-permute-start.8
  25.9 1.1 %fusion.1 = (f32[2,64,512]{2,1,0:T(8,128)S(1)}, f32[2,64,512]{2,1,0:T(8,128)S(1)}) fusion(f32[8,256,512]{2,1,0:T(8,128)} %c_ref.9), kind=kLoop, calls=%fused_computation.1 | loop fusion | bytes 1048576 | tf_op jit(solution)/shard_map/slice | solution.py:437
  27.0 1.2 %collective-permute-start.3 = (f32[2,64,512]{2,1,0:T(8,128)S(1)}, f32[2,64,512]{2,1,0:T(8,128)S(1)}, u32[]{:S(2)}, u32[]{:S(2)}) collective-permute-start(f32[2,64,512]{2,1,0:T(8,128)S(1)} %get-tuple-element.123), channel_id=1, source_target_pairs={{0,1},{1,2},{2,3},{3,0},{4,5},{5,6},{6,7},{7,4},{8,9},{9,10},{10,1... | collective-permute-start | bytes 786440 | tf_op jit(solution)/shard_map/ppermute | solution.py:26
  28.2 2.7 %collective-permute-start.4 = (f32[2,64,512]{2,1,0:T(8,128)S(1)}, f32[2,64,512]{2,1,0:T(8,128)S(1)}, u32[]{:S(2)}, u32[]{:S(2)}) collective-permute-start(f32[2,64,512]{2,1,0:T(8,128)S(1)} %get-tuple-element.122), channel_id=1, source_target_pairs={{0,3},{1,0},{2,1},{3,2},{4,7},{5,4},{6,5},{7,6},{8,11},{9,8},{10,9... | collective-permute-start | bytes 786440 | tf_op jit(solution)/shard_map/ppermute | solution.py:26
  30.9 0.0 collective-permute-done.5.refs_1_
  30.9 0.5 smooth_z.1
  31.3 6.8 %collective-permute-done.3.before_ref = f32[2,64,512]{2,1,0:T(8,128)S(1)} collective-permute-done((f32[2,64,512]{2,1,0:T(8,128)S(1)}, f32[2,64,512]{2,1,0:T(8,128)S(1)}, u32[]{:S(2)}, u32[]{:S(2)}) %collective-permute-start.3) | collective-permute-done | bytes 262176 | tf_op jit(solution)/shard_map/ppermute | solution.py:26
  38.1 3.4 %collective-permute-done.4.after_ref = f32[2,64,512]{2,1,0:T(8,128)S(1)} collective-permute-done((f32[2,64,512]{2,1,0:T(8,128)S(1)}, f32[2,64,512]{2,1,0:T(8,128)S(1)}, u32[]{:S(2)}, u32[]{:S(2)}) %collective-permute-start.4) | collective-permute-done | bytes 262176 | tf_op jit(solution)/shard_map/ppermute | solution.py:26
  41.5 2.7 %smooth_yx_short.3.refs_0_ = f32[233,8,128]{2,1,0:T(8,128)S(1)} custom-call(f32[2,64,512]{2,1,0:T(8,128)S(1)} %collective-permute-done.3.before_ref, f32[8,256,512]{2,1,0:T(8,128)} %c_ref.9, f32[2,64,512]{2,1,0:T(8,128)S(1)} %collective-permute-done.4.after_ref), custom_call_target="tpu_custom_call" | custom-call | flops 6963200 | bytes 3481600 | tf_op jit(solution)/shard_map/smooth_yx_short/pallas_call | solution.py:395
  44.2 1.6 %collective-permute-start.11 = (f32[233,8,128]{2,1,0:T(8,128)S(1)}, f32[233,8,128]{2,1,0:T(8,128)S(1)}, u32[]{:S(2)}, u32[]{:S(2)}) collective-permute-start(f32[233,8,128]{2,1,0:T(8,128)S(1)} %smooth_yx_short.3.refs_0_), channel_id=1, source_target_pairs={{0,16},{4,20},{8,24},{12,28},{16,0},{20,4},{24,8},{28,12},{1,17},{... | collective-permute-start | bytes 2863112 | tf_op jit(solution)/shard_map/ppermute | solution.py:26
  45.8 1.1 %fusion = (f32[2,64,512]{2,1,0:T(8,128)S(1)}, f32[2,64,512]{2,1,0:T(8,128)S(1)}) fusion(f32[8,256,512]{2,1,0:T(8,128)} %c_ref.9), kind=kLoop, calls=%fused_computation | loop fusion | bytes 1048576 | tf_op jit(solution)/shard_map/slice | solution.py:437
  46.9 0.4 collective-permute-start.6
  47.3 3.5 %collective-permute-start.7 = (f32[2,64,512]{2,1,0:T(8,128)S(1)}, f32[2,64,512]{2,1,0:T(8,128)S(1)}, u32[]{:S(2)}, u32[]{:S(2)}) collective-permute-start(f32[2,64,512]{2,1,0:T(8,128)S(1)} %get-tuple-element.120), channel_id=1, source_target_pairs={{0,3},{1,0},{2,1},{3,2},{4,7},{5,4},{6,5},{7,6},{8,11},{9,8},{10,9... | collective-permute-start | bytes 786440 | tf_op jit(solution)/shard_map/ppermute | solution.py:26
  50.8 0.0 copy-start
  50.8 0.3 collective-permute-start.10
  51.1 6.8 %collective-permute-done.6.before_ref = f32[2,64,512]{2,1,0:T(8,128)S(1)} collective-permute-done((f32[2,64,512]{2,1,0:T(8,128)S(1)}, f32[2,64,512]{2,1,0:T(8,128)S(1)}, u32[]{:S(2)}, u32[]{:S(2)}) %collective-permute-start.6) | collective-permute-done | bytes 262176 | tf_op jit(solution)/shard_map/ppermute | solution.py:26
  58.0 4.0 %collective-permute-done.7.after_ref = f32[2,64,512]{2,1,0:T(8,128)S(1)} collective-permute-done((f32[2,64,512]{2,1,0:T(8,128)S(1)}, f32[2,64,512]{2,1,0:T(8,128)S(1)}, u32[]{:S(2)}, u32[]{:S(2)}) %collective-permute-start.7) | collective-permute-done | bytes 262176 | tf_op jit(solution)/shard_map/ppermute | solution.py:26
  62.0 0.0 collective-permute-done.8.refs_1_
  62.0 1.9 %smooth_yx.3.refs_0_ = f32[2,120,512]{2,1,0:T(8,128)S(1)} custom-call(f32[2,64,512]{2,1,0:T(8,128)S(1)} %collective-permute-done.6.before_ref, f32[8,256,512]{2,1,0:T(8,128)} %c_ref.9, f32[2,64,512]{2,1,0:T(8,128)S(1)} %collective-permute-done.7.after_ref), custom_call_target="tpu_custom_call" | custom-call | flops 2555904 | bytes 1277952 | tf_op jit(solution)/shard_map/smooth_yx/pallas_call | solution.py:395
  63.9 0.6 collective-permute-start.15
  64.5 0.6 collective-permute-start.9
  65.1 1.9 %smooth_yx.2 = (f32[1,120,512]{2,1,0:T(8,128)S(1)}, f32[1,120,512]{2,1,0:T(8,128)S(1)}) custom-call(f32[2,64,512]{2,1,0:T(8,128)S(1)} %collective-permute-done.6.before_ref, f32[8,256,512]{2,1,0:T(8,128)} %c_ref.9, f32[2,64,512]{2,1,0:T(8,128)S(1)} %collective-permute-done.7.after_ref), custom_call_target="tpu_custom_call" | custom-call | flops 2555904 | bytes 1277952 | tf_op jit(solution)/shard_map/smooth_yx/pallas_call | solution.py:395
  67.0 1.5 %collective-permute-start.16 = (f32[1,120,512]{2,1,0:T(8,128)S(1)}, f32[1,120,512]{2,1,0:T(8,128)S(1)}, u32[]{:S(2)}, u32[]{:S(2)}) collective-permute-start(f32[1,120,512]{2,1,0:T(8,128)S(1)} %get-tuple-element.108.refs_0_), channel_id=1, source_target_pairs={{0,16},{4,20},{8,24},{12,28},{16,0},{20,4},{24,8},{28,12},{1,17},{... | collective-permute-start | bytes 737288 | tf_op jit(solution)/shard_map/ppermute | solution.py:26
  68.5 0.0 collective-permute-done.10.after_ref
  68.5 0.5 collective-permute-start.17
  69.1 4.0 %collective-permute-done.9.before_ref = f32[2,64,512]{2,1,0:T(8,128)S(1)} collective-permute-done((f32[2,64,512]{2,1,0:T(8,128)S(1)}, f32[2,64,512]{2,1,0:T(8,128)S(1)}, u32[]{:S(2)}, u32[]{:S(2)}) %collective-permute-start.9) | collective-permute-done | bytes 262176 | tf_op jit(solution)/shard_map/ppermute | solution.py:26
  73.1 0.0 copy-done
  73.1 1.4 %smooth_y.1 = (f32[8,256,512]{2,1,0:T(8,128)}, f32[8,256,512]{2,1,0:T(8,128)}) custom-call(f32[2,64,512]{2,1,0:T(8,128)S(1)} %collective-permute-done.9.before_ref, f32[2,256,512]{2,1,0:T(8,128)S(1)} %bitcast.12, f32[2,64,512]{2,1,0:T(8,128)S(1)} %collective-permute-done.10.after_ref, f32[8,256,512]{2,1,0:T(8,128)S(1)} %copy-done), custom_call_target="tpu_custom_call" | custom-call | flops 9437184 | bytes 4718592 | tf_op jit(solution)/shard_map/smooth_y/pallas_call | solution.py:395
  74.6 0.0 collective-permute-done.11.refs_1_
  74.6 0.7 smooth_z_short.2
  75.3 0.7 smooth_z_short.3
  75.9 0.1 collective-permute-start.12
  76.0 0.8 collective-permute-start.13
  76.8 5.3 %collective-permute-done.12.refs_0_ = f32[4,8,512]{2,1,0:T(8,128)S(1)} collective-permute-done((f32[4,8,512]{2,1,0:T(8,128)S(1)}, f32[4,8,512]{2,1,0:T(8,128)S(1)}, u32[]{:S(2)}, u32[]{:S(2)}) %collective-permute-start.12) | collective-permute-done | bytes 65568 | tf_op jit(solution)/shard_map/ppermute | solution.py:26
  82.1 0.0 collective-permute-start.14
  82.1 0.0 collective-permute-done.13.refs_1_
  82.1 4.3 %collective-permute-done.14.refs_2_ = f32[4,8,512]{2,1,0:T(8,128)S(1)} collective-permute-done((f32[4,8,512]{2,1,0:T(8,128)S(1)}, f32[4,8,512]{2,1,0:T(8,128)S(1)}, u32[]{:S(2)}, u32[]{:S(2)}) %collective-permute-start.14) | collective-permute-done | bytes 65568 | tf_op jit(solution)/shard_map/ppermute | solution.py:26
  86.4 2.5 %finish_short.1 = (f32[8,256,512]{2,1,0:T(8,128)}, f32[8,256,512]{2,1,0:T(8,128)}) custom-call(f32[4,256,512]{2,1,0:T(8,128)S(1)} %get-tuple-element.88.whole_ref, f32[4,8,512]{2,1,0:T(8,128)S(1)} %collective-permute-done.12.refs_0_, f32[4,8,512]{2,1,0:T(8,128)S(1)} %collective-permute-done.13.refs_1_, ...), custom_call_target="tpu_custom_call", output_to_operand_aliasing={{0}: (5, {}), {1}: (6, {})} | custom-call | flops 17170432 | bytes 8585216 | tf_op jit(solution)/shard_map/finish_short/pallas_call | solution.py:395
  88.8 0.0 collective-permute-done.15.refs_1_
  88.8 1.3 %finish.2 = (f32[16,128,512]{2,1,0:T(8,128)}, f32[16,128,512]{2,1,0:T(8,128)}) custom-call(f32[2,120,512]{2,1,0:T(8,128)S(1)} %smooth_yx.3.refs_0_, f32[2,120,512]{2,1,0:T(8,128)S(1)} %collective-permute-done.15.refs_1_, f32[16,128,512]{2,1,0:T(8,128)S(1)} %bitcast.8, f32[16,128,512]{2,1,0:T(8,128)} %bitcast.13, ...), custom_call_target="tpu_custom_call", output_to_operand_aliasing={{0}: (3, {}), {1}: (4, {})} | custom-call | flops 5111808 | bytes 2555904 | tf_op jit(solution)/shard_map/finish/pallas_call | solution.py:395
  90.1 0.0 collective-permute-done.16.refs_1_
  90.1 1.0 %finish.3 = (f32[16,128,512]{2,1,0:T(8,128)}, f32[16,128,512]{2,1,0:T(8,128)}) custom-call(f32[1,120,512]{2,1,0:T(8,128)S(1)} %get-tuple-element.108.refs_0_, f32[1,120,512]{2,1,0:T(8,128)S(1)} %collective-permute-done.16.refs_1_, f32[16,128,512]{2,1,0:T(8,128)S(1)} %bitcast.9, ...), custom_call_target="tpu_custom_call", output_to_operand_aliasing={{0}: (3, {}), {1}: (4, {})} | custom-call | flops 2555904 | bytes 1277952 | tf_op jit(solution)/shard_map/finish/pallas_call | solution.py:395
  91.2 0.0 collective-permute-done.17.refs_1_
  91.2 1.0 %finish_last.1 = (f32[16,128,512]{2,1,0:T(8,128)}, f32[16,128,512]{2,1,0:T(8,128)}) custom-call(f32[1,120,512]{2,1,0:T(8,128)S(1)} %get-tuple-element.114.refs_0_, f32[1,120,512]{2,1,0:T(8,128)S(1)} %collective-permute-done.17.refs_1_, f32[16,128,512]{2,1,0:T(8,128)S(1)} %bitcast.10, ...), custom_call_target="tpu_custom_call", output_to_operand_aliasing={{0}: (3, {}), {1}: (4, {})} | custom-call | tf_op jit(solution)/shard_map/finish_last/pallas_call | solution.py:395
  (1 shorter events, 0.0 us)
Async XLA Ops:
  1.9 15.1 %collective-permute-start.2 = (f32[2,120,512]{2,1,0:T(8,128)S(1)}, f32[2,120,512]{2,1,0:T(8,128)S(1)}, u32[]{:S(2)}, u32[]{:S(2)}) collective-permute-start(f32[2,120,512]{2,1,0:T(8,128)S(1)} %pair_x.1.refs_0_), channel_id=1, source_target_pairs={{0,16},{4,20},{8,24},{12,28},{16,0},{20,4},{24,8},{28,12},{1,17},{... | collective-permute-start | bytes 1474568 | tf_op jit(solution)/shard_map/ppermute | solution.py:26
  7.9 11.1 %collective-permute-start = (f32[2,64,512]{2,1,0:T(8,128)S(1)}, f32[2,64,512]{2,1,0:T(8,128)S(1)}, u32[]{:S(2)}, u32[]{:S(2)}) collective-permute-start(f32[2,64,512]{2,1,0:T(8,128)S(1)} %get-tuple-element.125), channel_id=1, source_target_pairs={{0,1},{1,2},{2,3},{3,0},{4,5},{5,6},{6,7},{7,4},{8,9},{9,10},{10,1... | collective-permute-start | bytes 786440 | tf_op jit(solution)/shard_map/ppermute | solution.py:26
  9.6 13.1 %collective-permute-start.1 = (f32[2,64,512]{2,1,0:T(8,128)S(1)}, f32[2,64,512]{2,1,0:T(8,128)S(1)}, u32[]{:S(2)}, u32[]{:S(2)}) collective-permute-start(f32[2,64,512]{2,1,0:T(8,128)S(1)} %get-tuple-element.124), channel_id=1, source_target_pairs={{0,3},{1,0},{2,1},{3,2},{4,7},{5,4},{6,5},{7,6},{8,11},{9,8},{10,9... | collective-permute-start | bytes 786440 | tf_op jit(solution)/shard_map/ppermute | solution.py:26
  11.8 19.1 %collective-permute-start.5 = (f32[2,120,512]{2,1,0:T(8,128)S(1)}, f32[2,120,512]{2,1,0:T(8,128)S(1)}, u32[]{:S(2)}, u32[]{:S(2)}) collective-permute-start(f32[2,120,512]{2,1,0:T(8,128)S(1)} %smooth_x.1.refs_0_), channel_id=1, source_target_pairs={{0,16},{4,20},{8,24},{12,28},{16,0},{20,4},{24,8},{28,12},{1,17},{... | collective-permute-start | bytes 1474568 | tf_op jit(solution)/shard_map/ppermute | solution.py:26
  25.4 36.6 %collective-permute-start.8 = (f32[233,8,128]{2,1,0:T(8,128)S(1)}, f32[233,8,128]{2,1,0:T(8,128)S(1)}, u32[]{:S(2)}, u32[]{:S(2)}) collective-permute-start(f32[233,8,128]{2,1,0:T(8,128)S(1)} %smooth_yx_short.2.refs_0_), channel_id=1, source_target_pairs={{0,16},{4,20},{8,24},{12,28},{16,0},{20,4},{24,8},{28,12},{1,17},{... | collective-permute-start | bytes 2863112 | tf_op jit(solution)/shard_map/ppermute | solution.py:26
  27.0 11.1 %collective-permute-start.3 = (f32[2,64,512]{2,1,0:T(8,128)S(1)}, f32[2,64,512]{2,1,0:T(8,128)S(1)}, u32[]{:S(2)}, u32[]{:S(2)}) collective-permute-start(f32[2,64,512]{2,1,0:T(8,128)S(1)} %get-tuple-element.123), channel_id=1, source_target_pairs={{0,1},{1,2},{2,3},{3,0},{4,5},{5,6},{6,7},{7,4},{8,9},{9,10},{10,1... | collective-permute-start | bytes 786440 | tf_op jit(solution)/shard_map/ppermute | solution.py:26
  28.2 13.3 %collective-permute-start.4 = (f32[2,64,512]{2,1,0:T(8,128)S(1)}, f32[2,64,512]{2,1,0:T(8,128)S(1)}, u32[]{:S(2)}, u32[]{:S(2)}) collective-permute-start(f32[2,64,512]{2,1,0:T(8,128)S(1)} %get-tuple-element.122), channel_id=1, source_target_pairs={{0,3},{1,0},{2,1},{3,2},{4,7},{5,4},{6,5},{7,6},{8,11},{9,8},{10,9... | collective-permute-start | bytes 786440 | tf_op jit(solution)/shard_map/ppermute | solution.py:26
  44.2 30.3 %collective-permute-start.11 = (f32[233,8,128]{2,1,0:T(8,128)S(1)}, f32[233,8,128]{2,1,0:T(8,128)S(1)}, u32[]{:S(2)}, u32[]{:S(2)}) collective-permute-start(f32[233,8,128]{2,1,0:T(8,128)S(1)} %smooth_yx_short.3.refs_0_), channel_id=1, source_target_pairs={{0,16},{4,20},{8,24},{12,28},{16,0},{20,4},{24,8},{28,12},{1,17},{... | collective-permute-start | bytes 2863112 | tf_op jit(solution)/shard_map/ppermute | solution.py:26
  46.9 11.1 %collective-permute-start.6 = (f32[2,64,512]{2,1,0:T(8,128)S(1)}, f32[2,64,512]{2,1,0:T(8,128)S(1)}, u32[]{:S(2)}, u32[]{:S(2)}) collective-permute-start(f32[2,64,512]{2,1,0:T(8,128)S(1)} %get-tuple-element.121), channel_id=1, source_target_pairs={{0,1},{1,2},{2,3},{3,0},{4,5},{5,6},{6,7},{7,4},{8,9},{9,10},{10,1... | collective-permute-start | bytes 786440 | tf_op jit(solution)/shard_map/ppermute | solution.py:26
  47.3 14.8 %collective-permute-start.7 = (f32[2,64,512]{2,1,0:T(8,128)S(1)}, f32[2,64,512]{2,1,0:T(8,128)S(1)}, u32[]{:S(2)}, u32[]{:S(2)}) collective-permute-start(f32[2,64,512]{2,1,0:T(8,128)S(1)} %get-tuple-element.120), channel_id=1, source_target_pairs={{0,3},{1,0},{2,1},{3,2},{4,7},{5,4},{6,5},{7,6},{8,11},{9,8},{10,9... | collective-permute-start | bytes 786440 | tf_op jit(solution)/shard_map/ppermute | solution.py:26
  50.8 22.3 %copy-start = (f32[8,256,512]{2,1,0:T(8,128)S(1)}, f32[8,256,512]{2,1,0:T(8,128)}, u32[]{:S(2)}) copy-start(f32[8,256,512]{2,1,0:T(8,128)} %c_ref.9) | copy-start | bytes 12582916
  50.8 17.8 %collective-permute-start.10 = (f32[2,64,512]{2,1,0:T(8,128)S(1)}, f32[2,64,512]{2,1,0:T(8,128)S(1)}, u32[]{:S(2)}, u32[]{:S(2)}) collective-permute-start(f32[2,64,512]{2,1,0:T(8,128)S(1)} %get-tuple-element.126), channel_id=1, source_target_pairs={{0,3},{1,0},{2,1},{3,2},{4,7},{5,4},{6,5},{7,6},{8,11},{9,8},{10,9... | collective-permute-start | bytes 786440 | tf_op jit(solution)/shard_map/ppermute | solution.py:26
  63.9 24.9 %collective-permute-start.15 = (f32[2,120,512]{2,1,0:T(8,128)S(1)}, f32[2,120,512]{2,1,0:T(8,128)S(1)}, u32[]{:S(2)}, u32[]{:S(2)}) collective-permute-start(f32[2,120,512]{2,1,0:T(8,128)S(1)} %smooth_yx.3.refs_0_), channel_id=1, source_target_pairs={{0,16},{4,20},{8,24},{12,28},{16,0},{20,4},{24,8},{28,12},{1,17},{... | collective-permute-start | bytes 1474568 | tf_op jit(solution)/shard_map/ppermute | solution.py:26
  64.5 8.6 %collective-permute-start.9 = (f32[2,64,512]{2,1,0:T(8,128)S(1)}, f32[2,64,512]{2,1,0:T(8,128)S(1)}, u32[]{:S(2)}, u32[]{:S(2)}) collective-permute-start(f32[2,64,512]{2,1,0:T(8,128)S(1)} %get-tuple-element.127), channel_id=1, source_target_pairs={{0,1},{1,2},{2,3},{3,0},{4,5},{5,6},{6,7},{7,4},{8,9},{9,10},{10,1... | collective-permute-start | bytes 786440 | tf_op jit(solution)/shard_map/ppermute | solution.py:26
  67.0 23.1 %collective-permute-start.16 = (f32[1,120,512]{2,1,0:T(8,128)S(1)}, f32[1,120,512]{2,1,0:T(8,128)S(1)}, u32[]{:S(2)}, u32[]{:S(2)}) collective-permute-start(f32[1,120,512]{2,1,0:T(8,128)S(1)} %get-tuple-element.108.refs_0_), channel_id=1, source_target_pairs={{0,16},{4,20},{8,24},{12,28},{16,0},{20,4},{24,8},{28,12},{1,17},{... | collective-permute-start | bytes 737288 | tf_op jit(solution)/shard_map/ppermute | solution.py:26
  68.5 22.6 %collective-permute-start.17 = (f32[1,120,512]{2,1,0:T(8,128)S(1)}, f32[1,120,512]{2,1,0:T(8,128)S(1)}, u32[]{:S(2)}, u32[]{:S(2)}) collective-permute-start(f32[1,120,512]{2,1,0:T(8,128)S(1)} %get-tuple-element.114.refs_0_), channel_id=1, source_target_pairs={{0,16},{4,20},{8,24},{12,28},{16,0},{20,4},{24,8},{28,12},{1,17},{... | collective-permute-start | bytes 737288 | tf_op jit(solution)/shard_map/ppermute | solution.py:26
  75.9 6.2 %collective-permute-start.12 = (f32[4,8,512]{2,1,0:T(8,128)S(1)}, f32[4,8,512]{2,1,0:T(8,128)S(1)}, u32[]{:S(2)}, u32[]{:S(2)}) collective-permute-start(f32[4,8,512]{2,1,0:T(8,128)S(1)} %get-tuple-element.91), channel_id=1, source_target_pairs={{0,1},{1,2},{2,3},{3,0},{4,5},{5,6},{6,7},{7,4},{8,9},{9,10},{10,1... | collective-permute-start | bytes 196616 | tf_op jit(solution)/shard_map/ppermute | solution.py:26
  76.0 6.1 %collective-permute-start.13 = (f32[4,8,512]{2,1,0:T(8,128)S(1)}, f32[4,8,512]{2,1,0:T(8,128)S(1)}, u32[]{:S(2)}, u32[]{:S(2)}) collective-permute-start(f32[4,8,512]{2,1,0:T(8,128)S(1)} %get-tuple-element.92), channel_id=1, source_target_pairs={{0,2},{1,3},{2,0},{3,1},{4,6},{5,7},{6,4},{7,5},{8,10},{9,11},{10,... | collective-permute-start | bytes 196616 | tf_op jit(solution)/shard_map/ppermute | solution.py:26
  82.1 4.3 %collective-permute-start.14 = (f32[4,8,512]{2,1,0:T(8,128)S(1)}, f32[4,8,512]{2,1,0:T(8,128)S(1)}, u32[]{:S(2)}, u32[]{:S(2)}) collective-permute-start(f32[4,8,512]{2,1,0:T(8,128)S(1)} %get-tuple-element.93), channel_id=1, source_target_pairs={{0,3},{1,0},{2,1},{3,2},{4,7},{5,4},{6,5},{7,6},{8,11},{9,8},{10,9... | collective-permute-start | bytes 196616 | tf_op jit(solution)/shard_map/ppermute | solution.py:26
where the time goes:
time: 92.5 us; the launch traced here: 92.2 us
  waiting for transfers between devices  44 us (48%)
  Pallas kernels  22.6 us (24%)
  starting transfers between devices  21.6 us (23%)
  local copies, waits for them, and re-layouts  3.25 us (4%)
    ppermute x18, waiting for transfers between devices, passed_along(): return lax.ppermute(x, axis, [(i, (i + by) % peers) for i in range(peers)])  44 us
    pallas_call x15, Pallas kernels, call(): pl.pallas_call(kernel, grid=(steps,) if steps else (), in_specs=in_specs,...  22.6 us
    ppermute x18, starting transfers between devices, passed_along(): return lax.ppermute(x, axis, [(i, (i + by) % peers) for i in range(peers)])  21.6 us
    slice x4, local copies, waits for them, and re-layouts, halo(): source[start:stop, :REACH]  3.24 us
  transfers between devices with their start and end apart: 18, of which 10 were waited for; matrix products, arithmetic and copies ran while one was open for 4% of the time, Pallas kernels for 22%

commit v1 on v0

--- a/solution.py
+++ b/solution.py
@@ -13,10 +13,8 @@
 LANES = 128
 STRIP = 8
 UNIT_ROWS = 128
-FIRST_PLANES = 2
-LEAD_UNITS = 2
-LATER_GROUPS = (((2, 0),), ((2, 0),), ((1, 1), (1, 2)))
-SHORT_FIRST = 2
+FIRST_PLANES = 3
+LATER_GROUPS = ((2, ()), (1, ()), (2, (2, 1, 1)))
 
 kernel_weights = (0.0625, 0.25, 0.375, 0.25, 0.0625)
 
@@ -75,8 +73,8 @@
     return high + middle + low
 
 
-def y_sums(groups):
-    for _ in range(4):
+def y_sums(groups, factors=4):
+    for _ in range(factors):
         groups = [a + b for a, b in zip(groups[:-1], groups[1:])]
     return groups
 
@@ -156,25 +154,9 @@
         store_packed(out_ref, unit, pair_sums(read_ref[unit]))
 
 
-def x_kernel(first, units_ref, out_ref, read_ref, matrix_ref, read_sems):
-    count = out_ref.shape[0]
-
-    def read(unit):
-        return pltpu.make_async_copy(units_ref.at[first + unit], read_ref.at[unit], read_sems.at[unit])
-
-    for unit in range(count):
-        read(unit).start()
-    fill_matrix(matrix_ref, x_taps())
-
-    @pl.loop(0, count)
-    def _(unit):
-        read(unit).wait()
-        store_packed(out_ref, unit, x_smoothed(read_ref[unit], matrix_ref[...]))
-
-
-def extended_groups(before_ref, c_ref, after_ref, offset):
+def extended_groups(refs, offset):
     groups = []
-    for ref in (before_ref, c_ref, after_ref):
+    for ref in refs:
         for start in range(0, ref.shape[1], TAP_DILATION):
             groups.append(ref[0, pl.ds(start + offset, STRIP), :])
     return groups
@@ -182,28 +164,29 @@
 
 def y_smoothed(before_ref, c_ref, after_ref, smooth_ref):
     for within in range(TAP_DILATION // STRIP):
-        groups = y_sums(extended_groups(before_ref, c_ref, after_ref, within * STRIP))
+        groups = y_sums(extended_groups((before_ref, c_ref, after_ref), within * STRIP))
         for group, strip in enumerate(groups):
             smooth_ref[pl.ds(group * TAP_DILATION + within * STRIP, STRIP), :] = strip * (1.0 / 16.0)
 
 
+def y_pairs(c_ref, after_ref, smooth_ref):
+    for within in range(TAP_DILATION // STRIP):
+        groups = extended_groups((c_ref, after_ref), within * STRIP)
+        for group, (strip, following) in enumerate(zip(groups[:-1], groups[1:])):
+            smooth_ref[pl.ds(group * TAP_DILATION + within * STRIP, STRIP), :] = (strip + following) * 0.5
+
+
 def yx_kernel(before_ref, c_ref, after_ref, *refs):
     *out_refs, matrix_ref, smooth_ref = refs
-    pl.when(pl.program_id(0) == 0)(lambda: fill_matrix(matrix_ref, x_taps()))
+    plane = pl.program_id(0)
+    pl.when(plane == 0)(lambda: fill_matrix(matrix_ref, x_taps()))
     y_smoothed(before_ref, c_ref, after_ref, smooth_ref)
-    places = [(ref, place) for ref in out_refs for place in range(ref.shape[0])]
-    for unit, (ref, place) in enumerate(places):
-        smooth = x_smoothed(smooth_ref[pl.ds(unit * UNIT_ROWS, UNIT_ROWS), :], matrix_ref[...])
-        store_packed(ref, place, smooth)
-
-
-def z_kernel(weights, *refs):
-    whole_ref = refs[-1]
-
-    def use(rows, strip):
-        whole_ref[0, rows, :] = strip
-
-    unpacked(weights, refs[: len(weights)], use)
+    parts = smooth_ref.shape[0] // UNIT_ROWS
+    for part in range(parts):
+        smooth = x_smoothed(smooth_ref[pl.ds(part * UNIT_ROWS, UNIT_ROWS), :], matrix_ref[...])
+        places = [(ref, place) for ref in out_refs for place in range(ref.shape[0])][part::parts]
+        for at, (ref, place) in enumerate(places):
+            pl.when(plane == at)(functools.partial(store_packed, ref, place, smooth))
 
 
 def group_of(shape):
@@ -233,7 +216,8 @@
     return (rows // STRIP - 3) * (width // LANES)
 
 
-def short_kernel(before_ref, c_ref, after_ref, out_ref, matrix_ref, smooth_ref):
+def short_kernel(filter_y, *refs):
+    *sources, out_ref, matrix_ref, smooth_ref = refs
     plane = pl.program_id(0)
 
     @pl.when(plane == 0)
@@ -241,7 +225,7 @@
         fill_matrix(matrix_ref, x_taps())
         out_ref[out_ref.shape[0] - 1] = jnp.zeros((STRIP, LANES), jnp.float32)
 
-    y_smoothed(before_ref, c_ref, after_ref, smooth_ref)
+    filter_y(*sources, smooth_ref)
     rows, width = smooth_ref.shape
     for start in range(0, rows, UNIT_ROWS):
         unit = pl.ds(start, UNIT_ROWS)
@@ -327,15 +311,23 @@
     whole_ref[0] = x_smoothed(pair_ref[...], matrix_ref[...])
 
 
-def y_kernel(before_ref, whole_ref, after_ref, c_ref, detail_ref, coarse_ref):
-    scale = 1.0 / 16.0
+def y_kernel(factors, before_ref, whole_ref, after_ref, c_ref, *refs):
+    detail_ref, coarse_ref = refs[-2:]
+    scale = 0.5**factors
     for within in range(TAP_DILATION // STRIP):
-        groups = y_sums(extended_groups(before_ref, whole_ref, after_ref, within * STRIP))
-        for group, strip in enumerate(groups):
+        groups = y_sums(extended_groups((before_ref, whole_ref, after_ref), within * STRIP), factors)
+        for group in range(whole_ref.shape[1] // TAP_DILATION):
             rows = pl.ds(group * TAP_DILATION + within * STRIP, STRIP)
-            coarse = strip * scale
+            coarse = groups[group] * scale
             coarse_ref[0, rows, :] = coarse
             detail_ref[0, rows, :] = c_ref[0, rows, :] - coarse
+
+
+def complete_kernel(group_ref, *refs):
+    *sum_refs, out_ref = refs
+    missing = strip_rows(group_ref.shape[1], 0)
+    out_ref[...] = group_ref[...]
+    out_ref[0, missing, :] = group_ref[0, missing, :] + sum(ref[0] for ref in sum_refs)
 
 
 def finish_kernel(weights, *refs):
@@ -381,8 +373,8 @@
     return pl.BlockSpec(memory_space=pl.ANY)
 
 
-def tiles_of(pieces):
-    return pl.BlockSpec((pieces, STRIP, LANES), lambda step: (0, 0, 0))
+def all_of(*shape):
+    return pl.BlockSpec(shape, lambda step: (0, 0, 0))
 
 
 def in_vmem():
@@ -421,14 +413,17 @@
 
 def shards(coarse_six):
     planes, rows, width = coarse_six.shape
+    assert can_shorten(rows, width)
     short = packed_rows(width)
     own, shifts = z_taps(planes, lax.axis_size("gz"))
     weights = (own, *shifts.values())
     count = len(weights)
     whole, unit, packed, edge = (functools.partial(block_of, n, width) for n in (rows, UNIT_ROWS, short, REACH))
+    strip = functools.partial(block_of, STRIP, width)
     parts = rows // UNIT_ROWS
     units = coarse_six.reshape(planes * parts, UNIT_ROWS, width)
     matrix = pltpu.VMEM((width, width), jnp.bfloat16)
+    smooth = pltpu.VMEM((rows, width), jnp.float32)
 
     def along_gz(x):
         return [passed_along(x, "gz", moved) for moved in shifts]
@@ -437,158 +432,142 @@
         top, bottom = source[start:stop, :REACH], source[start:stop, rows - REACH :]
         return passed_along(bottom, "gy", 1), passed_along(top, "gy", -1)
 
-    sums_shape = f32(FIRST_PLANES * parts, UNIT_ROWS, width)
+    def send_short(filter_y, size, specs, sources):
+        pieces = size * short_tiles(rows, width) + 1
+        block = call(
+            functools.partial(short_kernel, filter_y),
+            "smooth_yx_short",
+            size,
+            specs,
+            [all_of(pieces, STRIP, LANES)],
+            [f32(pieces, STRIP, LANES)],
+            sources,
+            scratch=[matrix, smooth],
+        )[0]
+        return block, *along_gz(block)
+
+    def sum_short(batch, into=(), first=0):
+        size_of_all = sum(size for _, size, _ in batch)
+        whole_shape = into[0].shape if into else (size_of_all, rows, width)
+        step, sums = 0, list(into)
+        for _, size, blocks in batch:
+            sums = call(
+                functools.partial(short_z_kernel, weights),
+                "smooth_z_short",
+                size,
+                [all_of(*blocks[0].shape)] * count + [anywhere()] * len(sums),
+                [whole(first + step)] + [strip(step)] * 3,
+                [f32(*whole_shape)] + [f32(size_of_all, STRIP, width)] * 3,
+                [*blocks, *sums],
+                {count + at: at for at in range(len(sums))},
+            )
+            step += size
+        return sums[0], [passed_along(total, "gy", ahead) for ahead, total in enumerate(sums[1:], 1)]
+
     lead = call(
         pair_kernel,
         "pair_x",
         0,
         [anywhere()],
         [in_vmem()],
-        [pltpu.VMEM((LEAD_UNITS, short, width), jnp.float32)],
+        [pltpu.VMEM((parts, short, width), jnp.float32)],
         [in_hbm(units)],
-        scratch=[pltpu.VMEM((LEAD_UNITS, UNIT_ROWS, width), jnp.float32), pltpu.SemaphoreType.DMA((LEAD_UNITS,))],
+        scratch=[pltpu.VMEM((parts, UNIT_ROWS, width), jnp.float32), pltpu.SemaphoreType.DMA((parts,))],
     )[0]
-    lead, ready = lax.optimization_barrier((lead, units))
+    lead, ready = lax.optimization_barrier((lead, coarse_six))
     lead_moved = along_gz(lead)
-    first = FIRST_PLANES * parts - LEAD_UNITS
-    first_block = call(
-        functools.partial(x_kernel, LEAD_UNITS),
-        "smooth_x",
-        0,
-        [anywhere()],
-        [in_vmem()],
-        [pltpu.VMEM((first, short, width), jnp.float32)],
-        [in_hbm(ready)],
-        scratch=[
-            pltpu.VMEM((first, UNIT_ROWS, width), jnp.float32),
-            matrix,
-            pltpu.SemaphoreType.DMA((first,)),
-        ],
-    )[0]
-    first_block, ready = lax.optimization_barrier((first_block, coarse_six))
-    first_moved = along_gz(first_block)
+    others = FIRST_PLANES - 1
+    following = passed_along(ready[1:FIRST_PLANES, :TAP_DILATION], "gy", -1)
+    first_sent = send_short(
+        y_pairs, others, [whole(1), block_of(TAP_DILATION, width)], [in_hbm(coarse_six), following]
+    )
     sums = call(
         functools.partial(pair_z_kernel, weights),
         "smooth_zx",
-        LEAD_UNITS,
+        parts,
         [packed()] * count,
         [unit()],
-        [sums_shape],
+        [f32(FIRST_PLANES * parts, UNIT_ROWS, width)],
         [lead, *lead_moved],
         scratch=[matrix, pltpu.VMEM((UNIT_ROWS, width), jnp.float32)],
-    )
+    )[0]
 
     later, short_sent = [], []
     start = FIRST_PLANES
-    near = halo(ready, start, start + sum(size for size, _ in LATER_GROUPS[0]))
+    lead_moved, ready = lax.optimization_barrier((lead_moved, ready))
+    near = halo(ready, start, start + LATER_GROUPS[0][0])
     near, sums = lax.optimization_barrier((near, sums))
-    for number, sizes in enumerate(LATER_GROUPS):
-        offset = 0
-        for size, messages in sizes:
-            place = start + offset
-            sources = [near[0], in_hbm(coarse_six), near[1]]
-            specs = [edge(offset), whole(place), edge(offset)]
-            scratch = [matrix, pltpu.VMEM((rows, width), jnp.float32)]
-            if messages or not can_shorten(rows, width):
-                messages = max(messages, 1)
-                depth = parts // messages
-                blocks = call(
-                    yx_kernel,
-                    "smooth_yx",
-                    size,
-                    specs,
-                    [packed(depth=depth)] * messages,
-                    [f32(size * depth, short, width)] * messages,
-                    sources,
-                    scratch=scratch,
-                )
-                for message, block in enumerate(blocks):
-                    later.append((place * parts + message * depth, size * depth, (block, *along_gz(block))))
-            else:
-                pieces = size * short_tiles(rows, width) + 1
-                block = call(
-                    short_kernel,
-                    "smooth_yx_short",
-                    size,
-                    specs,
-                    [tiles_of(pieces)],
-                    [f32(pieces, STRIP, LANES)],
-                    sources,
-                    scratch=scratch,
-                )[0]
-                short_sent.append((place, size, (block, *along_gz(block))))
-            offset += size
-        start += offset
+    for number, (size, messages) in enumerate(LATER_GROUPS):
+        sources = [near[0], in_hbm(coarse_six), near[1]]
+        specs = [edge(), whole(start), edge()]
+        if messages:
+            blocks = call(
+                yx_kernel,
+                "smooth_yx",
+                size,
+                specs,
+                [all_of(length, short, width) for length in messages],
+                [f32(length, short, width) for length in messages],
+                sources,
+                scratch=[matrix, smooth],
+            )
+            place = start * parts
+            for block, length in zip(blocks, messages):
+                later.append((place, length, (block, *along_gz(block))))
+                place += length
+        else:
+            blocks = send_short(y_smoothed, size, specs, sources)
+            short_sent.append((start, size, blocks))
+            block = blocks[0]
+        start += size
+        if number == 1:
+            block, ready = lax.optimization_barrier((block, ready))
+            near = halo(ready, start, start + LATER_GROUPS[2][0])
         if number == 0:
             block, ready = lax.optimization_barrier((block, ready))
-            block, *first_moved = lax.optimization_barrier((block, *first_moved))
-            sums = call(
-                functools.partial(z_kernel, weights),
-                "smooth_z",
-                first,
-                [packed()] * count + [anywhere()],
-                [unit(LEAD_UNITS)],
-                [sums_shape],
-                [first_block, *first_moved, *sums],
-                {count: 0},
+            block, first_sent = lax.optimization_barrier((block, first_sent))
+            along_z, moved_sums = sum_short([(1, others, first_sent)], [sums.reshape(FIRST_PLANES, rows, width)], 1)
+            near = halo(ready, start, start + LATER_GROUPS[1][0])
+            near, along_z = lax.optimization_barrier((near, along_z))
+            last_group = pl.BlockSpec((1, TAP_DILATION, width), lambda step: (1 + step, rows // TAP_DILATION - 1, 0))
+            along_z = call(
+                complete_kernel,
+                "complete",
+                others,
+                [last_group] + [strip()] * 3,
+                [last_group],
+                [f32(*along_z.shape)],
+                [along_z, *moved_sums],
+                {0: 0},
             )[0]
-            along_z = sums.reshape(FIRST_PLANES, rows, width)
-        if number + 1 < len(LATER_GROUPS):
-            block, ready = lax.optimization_barrier((block, ready))
-            near = halo(ready, start, start + sum(size for size, _ in LATER_GROUPS[number + 1]))
-        if number and short_sent:
-            near, _ = lax.optimization_barrier((near, short_sent[0][2]))
-        if number == 0:
-            near, along_z = lax.optimization_barrier((near, along_z))
             sides = halo(along_z, 0, FIRST_PLANES)
 
-    def sum_short(batch):
-        planes_in = sum(size for _, size, _ in batch)
-        step, sums = 0, []
-        for _, size, blocks in batch:
-            sums = call(
-                functools.partial(short_z_kernel, weights),
-                "smooth_z_short",
-                size,
-                [tiles_of(blocks[0].shape[0])] * count + [anywhere()] * len(sums),
-                [whole(step)] + [block_of(STRIP, width, step)] * 3,
-                [f32(planes_in, rows, width)] + [f32(planes_in, STRIP, width)] * 3,
-                [*blocks, *sums],
-                {count + at: at for at in range(len(sums))},
-            )
-            step += size
-        return sums[0], [passed_along(total, "gy", ahead) for ahead, total in enumerate(sums[1:], 1)]
-
-    def finish_short(batch, sums, outs):
-        start, size = batch[0][0], sum(size for _, size, _ in batch)
-        along_z, moved = sums
-        outs, moved = lax.optimization_barrier((outs, moved))
-        return call(
-            short_finish_kernel,
-            "finish_short",
+    short_sums = sum_short(short_sent)
+    short_whole, sides = lax.optimization_barrier((short_sums[0], sides))
+    outs = ()
+    for place, size, factors in ((0, 1, 4), (1, others, 3)):
+        outs = call(
+            functools.partial(y_kernel, factors),
+            "smooth_y",
             size,
-            [whole()] + [block_of(STRIP, width)] * 3 + [whole(start)] + [anywhere()] * 2,
-            [whole(start)] * 2,
+            [edge(place), whole(place), edge(place), whole(place)] + [anywhere()] * len(outs),
+            [whole(place)] * 2,
             [f32(planes, rows, width)] * 2,
-            [along_z, *moved, coarse_six, *outs],
-            {5: 0, 6: 1},
+            [sides[0], along_z, sides[1], coarse_six, *outs],
+            {4 + at: at for at in range(len(outs))},
         )
-
-    batches = [batch for batch in (short_sent[:SHORT_FIRST], short_sent[SHORT_FIRST:]) if batch]
-    block, sides = lax.optimization_barrier((block, sides))
+    outs, moved_sums = lax.optimization_barrier((outs, short_sums[1]))
+    place = short_sent[0][0]
     outs = call(
-        y_kernel,
-        "smooth_y",
-        FIRST_PLANES,
-        [edge(), whole(), edge(), whole()],
-        [whole(), whole()],
+        short_finish_kernel,
+        "finish_short",
+        sum(size for _, size, _ in short_sent),
+        [whole()] + [strip()] * 3 + [whole(place)] + [anywhere()] * 2,
+        [whole(place)] * 2,
         [f32(planes, rows, width)] * 2,
-        [sides[0], along_z, sides[1], coarse_six],
+        [short_whole, *moved_sums, coarse_six, *outs],
+        {5: 0, 6: 1},
     )
-    for batch in batches:
-        outs, blocks = lax.optimization_barrier((outs, [blocks for _, _, blocks in batch]))
-        sums = sum_short([(place, size, block) for (place, size, _), block in zip(batch, blocks)])
-        outs = finish_short(batch, sums, outs)
     outs = [out.reshape(units.shape) for out in outs]
     for place, size, blocks in later[:-1]:
         outs, blocks = lax.optimization_barrier((outs, blocks))

time: 92.5 us -> 95.6 us (1.034)
  starting transfers between devices: 21.6 us -> 34.5 us
  waiting for transfers between devices: 44 us -> 33.2 us
    ppermute x18 -> x22, starting transfers between devices: 21.6 us -> 34.5 us  [passed_along(): return lax.ppermute(x, axis, [(i, (i + by) % peers) for i in range(peers)])]
    ppermute x18 -> x22, waiting for transfers between devices: 44 us -> 33.2 us  [passed_along(): return lax.ppermute(x, axis, [(i, (i + by) % peers) for i in range(peers)])]
    pallas_call x15 -> x16, Pallas kernels: 22.6 us -> 22.7 us  [call(): pl.pallas_call(kernel, grid=(steps,) if steps else (), in_specs=in_specs,...]
  transfers between devices with their start and end apart: 18 -> 22, of which waited for: 10 -> 9; matrix products, arithmetic and copies ran while one was open for 4% -> 4% of each run, Pallas kernels for 22% -> 21%
where the time goes in v1:
time: 95.6 us; the launch traced here: 95.3 us
  starting transfers between devices  34.5 us (36%)
  waiting for transfers between devices  33.2 us (35%)
  Pallas kernels  22.7 us (24%)
  local copies, waits for them, and re-layouts  4.1 us (4%)
    ppermute x22, starting transfers between devices, passed_along(): return lax.ppermute(x, axis, [(i, (i + by) % peers) for i in range(peers)])  34.5 us
    ppermute x22, waiting for transfers between devices, passed_along(): return lax.ppermute(x, axis, [(i, (i + by) % peers) for i in range(peers)])  33.2 us
    pallas_call x16, Pallas kernels, call(): pl.pallas_call(kernel, grid=(steps,) if steps else (), in_specs=in_specs,...  22.7 us
    slice x4, local copies, waits for them, and re-layouts, halo(): source[start:stop, :REACH]  3.18 us
  transfers between devices with their start and end apart: 22, of which 9 were waited for; matrix products, arithmetic and copies ran while one was open for 4% of the time, Pallas kernels for 21%

profile of v1, /device:TPU:0, one launch (start us, length us, event | category | flops | bytes accessed | tf_op | source)
XLA Modules:
  0.0 95.3 jit_solution(9113549911398268724)
XLA Ops:
  0.6 1.3 %pair_x.1.refs_0_ = f32[2,120,512]{2,1,0:T(8,128)S(1)} custom-call(f32[16,128,512]{2,1,0:T(8,128)} %bitcast.6), custom_call_target="tpu_custom_call" | custom-call | tf_op jit(solution)/shard_map/pair_x/pallas_call | solution.py:387
  1.9 3.0 %collective-permute-start = (f32[2,120,512]{2,1,0:T(8,128)S(1)}, f32[2,120,512]{2,1,0:T(8,128)S(1)}, u32[]{:S(2)}, u32[]{:S(2)}) collective-permute-start(f32[2,120,512]{2,1,0:T(8,128)S(1)} %pair_x.1.refs_0_), channel_id=1, source_target_pairs={{0,16},{4,20},{8,24},{12,28},{16,0},{20,4},{24,8},{28,12},{1,17},{... | collective-permute-start | bytes 1474568 | tf_op jit(solution)/shard_map/ppermute | solution.py:24
  5.0 0.9 slice.31
  5.9 3.7 %collective-permute-start.5 = (f32[2,32,512]{2,1,0:T(8,128)S(1)}, f32[2,32,512]{2,1,0:T(8,128)S(1)}, u32[]{:S(2)}, u32[]{:S(2)}) collective-permute-start(f32[2,32,512]{2,1,0:T(8,128)S(1)} %slice.31), channel_id=1, source_target_pairs={{0,3},{1,0},{2,1},{3,2},{4,7},{5,4},{6,5},{7,6},{8,11},{9,8},{10,9... | collective-permute-start | bytes 393224 | tf_op jit(solution)/shard_map/ppermute | solution.py:24
  9.5 2.5 %collective-permute-done.5.refs_1_ = f32[2,32,512]{2,1,0:T(8,128)S(1)} collective-permute-done((f32[2,32,512]{2,1,0:T(8,128)S(1)}, f32[2,32,512]{2,1,0:T(8,128)S(1)}, u32[]{:S(2)}, u32[]{:S(2)}) %collective-permute-start.5) | collective-permute-done | bytes 131104 | tf_op jit(solution)/shard_map/ppermute | solution.py:24
  12.1 2.7 %smooth_yx_short.4.refs_0_ = f32[233,8,128]{2,1,0:T(8,128)S(1)} custom-call(f32[8,256,512]{2,1,0:T(8,128)} %c_ref.5, f32[2,32,512]{2,1,0:T(8,128)S(1)} %collective-permute-done.5.refs_1_), custom_call_target="tpu_custom_call" | custom-call | flops 6176768 | bytes 3088384 | tf_op jit(solution)/shard_map/smooth_yx_short/pallas_call | solution.py:387
  14.8 0.6 collective-permute-start.6
  15.3 1.3 %collective-permute-done.refs_1_ = f32[2,120,512]{2,1,0:T(8,128)S(1)} collective-permute-done((f32[2,120,512]{2,1,0:T(8,128)S(1)}, f32[2,120,512]{2,1,0:T(8,128)S(1)}, u32[]{:S(2)}, u32[]{:S(2)}) %collective-permute-start) | collective-permute-done | bytes 491552 | tf_op jit(solution)/shard_map/ppermute | solution.py:24
  16.6 1.1 %fusion.2 = (f32[2,64,512]{2,1,0:T(8,128)S(1)}, f32[2,64,512]{2,1,0:T(8,128)S(1)}) fusion(f32[8,256,512]{2,1,0:T(8,128)} %c_ref.5), kind=kLoop, calls=%fused_computation.2 | loop fusion | bytes 1048576 | tf_op jit(solution)/shard_map/slice | solution.py:432
  17.7 2.6 %collective-permute-start.1 = (f32[2,64,512]{2,1,0:T(8,128)S(1)}, f32[2,64,512]{2,1,0:T(8,128)S(1)}, u32[]{:S(2)}, u32[]{:S(2)}) collective-permute-start(f32[2,64,512]{2,1,0:T(8,128)S(1)} %get-tuple-element.127), channel_id=1, source_target_pairs={{0,1},{1,2},{2,3},{3,0},{4,5},{5,6},{6,7},{7,4},{8,9},{9,10},{10,1... | collective-permute-start | bytes 786440 | tf_op jit(solution)/shard_map/ppermute | solution.py:24
  20.2 1.3 %collective-permute-start.2 = (f32[2,64,512]{2,1,0:T(8,128)S(1)}, f32[2,64,512]{2,1,0:T(8,128)S(1)}, u32[]{:S(2)}, u32[]{:S(2)}) collective-permute-start(f32[2,64,512]{2,1,0:T(8,128)S(1)} %get-tuple-element.126), channel_id=1, source_target_pairs={{0,3},{1,0},{2,1},{3,2},{4,7},{5,4},{6,5},{7,6},{8,11},{9,8},{10,9... | collective-permute-start | bytes 786440 | tf_op jit(solution)/shard_map/ppermute | solution.py:24
  21.5 1.1 %smooth_zx.1 = f32[6,128,512]{2,1,0:T(8,128)S(1)} custom-call(f32[2,120,512]{2,1,0:T(8,128)S(1)} %pair_x.1.refs_0_, f32[2,120,512]{2,1,0:T(8,128)S(1)} %collective-permute-done.refs_1_), custom_call_target="tpu_custom_call" | custom-call | flops 3014656 | bytes 1507328 | tf_op jit(solution)/shard_map/smooth_zx/pallas_call | solution.py:387
  22.7 6.1 %collective-permute-done.1.refs_0_ = f32[2,64,512]{2,1,0:T(8,128)S(1)} collective-permute-done((f32[2,64,512]{2,1,0:T(8,128)S(1)}, f32[2,64,512]{2,1,0:T(8,128)S(1)}, u32[]{:S(2)}, u32[]{:S(2)}) %collective-permute-start.1) | collective-permute-done | bytes 262176 | tf_op jit(solution)/shard_map/ppermute | solution.py:24
  28.8 2.8 %collective-permute-done.2.refs_2_ = f32[2,64,512]{2,1,0:T(8,128)S(1)} collective-permute-done((f32[2,64,512]{2,1,0:T(8,128)S(1)}, f32[2,64,512]{2,1,0:T(8,128)S(1)}, u32[]{:S(2)}, u32[]{:S(2)}) %collective-permute-start.2) | collective-permute-done | bytes 262176 | tf_op jit(solution)/shard_map/ppermute | solution.py:24
  31.6 2.7 %smooth_yx_short.3.refs_0_ = f32[233,8,128]{2,1,0:T(8,128)S(1)} custom-call(f32[2,64,512]{2,1,0:T(8,128)S(1)} %collective-permute-done.1.refs_0_, f32[8,256,512]{2,1,0:T(8,128)} %c_ref.5, f32[2,64,512]{2,1,0:T(8,128)S(1)} %collective-permute-done.2.refs_2_), custom_call_target="tpu_custom_call" | custom-call | flops 6963200 | bytes 3481600 | tf_op jit(solution)/shard_map/smooth_yx_short/pallas_call | solution.py:387
  34.3 1.6 %collective-permute-start.8 = (f32[233,8,128]{2,1,0:T(8,128)S(1)}, f32[233,8,128]{2,1,0:T(8,128)S(1)}, u32[]{:S(2)}, u32[]{:S(2)}) collective-permute-start(f32[233,8,128]{2,1,0:T(8,128)S(1)} %smooth_yx_short.3.refs_0_), channel_id=1, source_target_pairs={{0,16},{4,20},{8,24},{12,28},{16,0},{20,4},{24,8},{28,12},{1,17},{... | collective-permute-start | bytes 2863112 | tf_op jit(solution)/shard_map/ppermute | solution.py:24
  35.9 1.0 %fusion.1 = (f32[1,64,512]{2,1,0:T(8,128)S(1)}, f32[1,64,512]{2,1,0:T(8,128)S(1)}) fusion(f32[8,256,512]{2,1,0:T(8,128)} %c_ref.5), kind=kLoop, calls=%fused_computation.1 | loop fusion | bytes 524288 | tf_op jit(solution)/shard_map/slice | solution.py:432
  36.9 1.2 %collective-permute-start.3 = (f32[1,64,512]{2,1,0:T(8,128)S(1)}, f32[1,64,512]{2,1,0:T(8,128)S(1)}, u32[]{:S(2)}, u32[]{:S(2)}) collective-permute-start(f32[1,64,512]{2,1,0:T(8,128)S(1)} %get-tuple-element.125), channel_id=1, source_target_pairs={{0,1},{1,2},{2,3},{3,0},{4,5},{5,6},{6,7},{7,4},{8,9},{9,10},{10,1... | collective-permute-start | bytes 393224 | tf_op jit(solution)/shard_map/ppermute | solution.py:24
  38.1 2.7 %collective-permute-start.4 = (f32[1,64,512]{2,1,0:T(8,128)S(1)}, f32[1,64,512]{2,1,0:T(8,128)S(1)}, u32[]{:S(2)}, u32[]{:S(2)}) collective-permute-start(f32[1,64,512]{2,1,0:T(8,128)S(1)} %get-tuple-element.124), channel_id=1, source_target_pairs={{0,3},{1,0},{2,1},{3,2},{4,7},{5,4},{6,5},{7,6},{8,11},{9,8},{10,9... | collective-permute-start | bytes 393224 | tf_op jit(solution)/shard_map/ppermute | solution.py:24
  40.8 0.0 collective-permute-done.6.refs_1_
  40.8 0.7 smooth_z_short.3
  41.5 3.4 %collective-permute-done.3.refs_0_ = f32[1,64,512]{2,1,0:T(8,128)S(1)} collective-permute-done((f32[1,64,512]{2,1,0:T(8,128)S(1)}, f32[1,64,512]{2,1,0:T(8,128)S(1)}, u32[]{:S(2)}, u32[]{:S(2)}) %collective-permute-start.3) | collective-permute-done | bytes 131104 | tf_op jit(solution)/shard_map/ppermute | solution.py:24
  44.8 0.2 collective-permute-done.4.refs_2_
  45.1 0.3 collective-permute-start.9
  45.4 3.1 %collective-permute-start.10 = (f32[2,8,512]{2,1,0:T(8,128)S(1)}, f32[2,8,512]{2,1,0:T(8,128)S(1)}, u32[]{:S(2)}, u32[]{:S(2)}) collective-permute-start(f32[2,8,512]{2,1,0:T(8,128)S(1)} %get-tuple-element.81), channel_id=1, source_target_pairs={{0,2},{1,3},{2,0},{3,1},{4,6},{5,7},{6,4},{7,5},{8,10},{9,11},{10,... | collective-permute-start | bytes 98312 | tf_op jit(solution)/shard_map/ppermute | solution.py:24
  48.5 1.1 %collective-permute-start.11 = (f32[2,8,512]{2,1,0:T(8,128)S(1)}, f32[2,8,512]{2,1,0:T(8,128)S(1)}, u32[]{:S(2)}, u32[]{:S(2)}) collective-permute-start(f32[2,8,512]{2,1,0:T(8,128)S(1)} %get-tuple-element.82), channel_id=1, source_target_pairs={{0,3},{1,0},{2,1},{3,2},{4,7},{5,4},{6,5},{7,6},{8,11},{9,8},{10,9... | collective-permute-start | bytes 98312 | tf_op jit(solution)/shard_map/ppermute | solution.py:24
  49.6 2.0 %smooth_yx_short.5.refs_0_ = f32[117,8,128]{2,1,0:T(8,128)S(1)} custom-call(f32[1,64,512]{2,1,0:T(8,128)S(1)} %collective-permute-done.3.refs_0_, f32[8,256,512]{2,1,0:T(8,128)} %c_ref.5, f32[1,64,512]{2,1,0:T(8,128)S(1)} %collective-permute-done.4.refs_2_), custom_call_target="tpu_custom_call" | custom-call | flops 2531328 | bytes 1265664 | tf_op jit(solution)/shard_map/smooth_yx_short/pallas_call | solution.py:387
  51.5 1.1 %fusion = (f32[2,64,512]{2,1,0:T(8,128)S(1)}, f32[2,64,512]{2,1,0:T(8,128)S(1)}) fusion(f32[8,256,512]{2,1,0:T(8,128)} %c_ref.5), kind=kLoop, calls=%fused_computation | loop fusion | bytes 1048576 | tf_op jit(solution)/shard_map/slice | solution.py:432
  52.6 1.0 %collective-permute-start.17 = (f32[2,64,512]{2,1,0:T(8,128)S(1)}, f32[2,64,512]{2,1,0:T(8,128)S(1)}, u32[]{:S(2)}, u32[]{:S(2)}) collective-permute-start(f32[2,64,512]{2,1,0:T(8,128)S(1)} %get-tuple-element.123), channel_id=1, source_target_pairs={{0,1},{1,2},{2,3},{3,0},{4,5},{5,6},{6,7},{7,4},{8,9},{9,10},{10,1... | collective-permute-start | bytes 786440 | tf_op jit(solution)/shard_map/ppermute | solution.py:24
  53.6 0.0 collective-permute-done.9.refs_0_
  53.6 2.9 %collective-permute-start.18 = (f32[2,64,512]{2,1,0:T(8,128)S(1)}, f32[2,64,512]{2,1,0:T(8,128)S(1)}, u32[]{:S(2)}, u32[]{:S(2)}) collective-permute-start(f32[2,64,512]{2,1,0:T(8,128)S(1)} %get-tuple-element.122), channel_id=1, source_target_pairs={{0,3},{1,0},{2,1},{3,2},{4,7},{5,4},{6,5},{7,6},{8,11},{9,8},{10,9... | collective-permute-start | bytes 786440 | tf_op jit(solution)/shard_map/ppermute | solution.py:24
  56.5 0.0 collective-permute-done.10.refs_1_
  56.5 0.5 collective-permute-start.7
  56.9 0.0 collective-permute-done.11.refs_2_
  57.0 0.1 fusion.3
  57.1 0.0 copy-start
  57.1 0.1 collective-permute-start.12
  57.2 6.7 %collective-permute-done.17.before_ref = f32[2,64,512]{2,1,0:T(8,128)S(1)} collective-permute-done((f32[2,64,512]{2,1,0:T(8,128)S(1)}, f32[2,64,512]{2,1,0:T(8,128)S(1)}, u32[]{:S(2)}, u32[]{:S(2)}) %collective-permute-start.17) | collective-permute-done | bytes 262176 | tf_op jit(solution)/shard_map/ppermute | solution.py:24
  63.8 3.7 %collective-permute-done.18.after_ref = f32[2,64,512]{2,1,0:T(8,128)S(1)} collective-permute-done((f32[2,64,512]{2,1,0:T(8,128)S(1)}, f32[2,64,512]{2,1,0:T(8,128)S(1)}, u32[]{:S(2)}, u32[]{:S(2)}) %collective-permute-start.18) | collective-permute-done | bytes 262176 | tf_op jit(solution)/shard_map/ppermute | solution.py:24
  67.5 3.2 %smooth_yx.1 = (f32[2,120,512]{2,1,0:T(8,128)S(1)}, f32[1,120,512]{2,1,0:T(8,128)S(1)}, f32[1,120,512]{2,1,0:T(8,128)S(1)}) custom-call(f32[2,64,512]{2,1,0:T(8,128)S(1)} %collective-permute-done.17.before_ref, f32[8,256,512]{2,1,0:T(8,128)} %c_ref.5, f32[2,64,512]{2,1,0:T(8,128)S(1)} %collective-permute-done.18.after_ref), custom_call_target="tpu_custom_call" | custom-call | flops 7077888 | bytes 3538944 | tf_op jit(solution)/shard_map/smooth_yx/pallas_call | solution.py:387
  70.7 0.1 collective-permute-start.19
  70.8 3.1 %collective-permute-start.13 = (f32[3,64,512]{2,1,0:T(8,128)S(1)}, f32[3,64,512]{2,1,0:T(8,128)S(1)}, u32[]{:S(2)}, u32[]{:S(2)}) collective-permute-start(f32[3,64,512]{2,1,0:T(8,128)S(1)} %get-tuple-element.128), channel_id=1, source_target_pairs={{0,3},{1,0},{2,1},{3,2},{4,7},{5,4},{6,5},{7,6},{8,11},{9,8},{10,9... | collective-permute-start | bytes 1179656 | tf_op jit(solution)/shard_map/ppermute | solution.py:24
  73.9 0.0 collective-permute-done.7.refs_1_
  73.9 1.7 %collective-permute-start.20 = (f32[1,120,512]{2,1,0:T(8,128)S(1)}, f32[1,120,512]{2,1,0:T(8,128)S(1)}, u32[]{:S(2)}, u32[]{:S(2)}) collective-permute-start(f32[1,120,512]{2,1,0:T(8,128)S(1)} %get-tuple-element.109.refs_0_), channel_id=1, source_target_pairs={{0,16},{4,20},{8,24},{12,28},{16,0},{20,4},{24,8},{28,12},{1,17},{... | collective-permute-start | bytes 737288 | tf_op jit(solution)/shard_map/ppermute | solution.py:24
  75.6 0.0 collective-permute-done.8.refs_1_
  75.6 0.4 collective-permute-start.21
  75.9 0.7 smooth_z_short.4
  76.6 0.3 smooth_z_short.5
  77.0 0.1 collective-permute-start.14
  77.0 6.4 %collective-permute-done.13.after_ref = f32[3,64,512]{2,1,0:T(8,128)S(1)} collective-permute-done((f32[3,64,512]{2,1,0:T(8,128)S(1)}, f32[3,64,512]{2,1,0:T(8,128)S(1)}, u32[]{:S(2)}, u32[]{:S(2)}) %collective-permute-start.13) | collective-permute-done | bytes 393248 | tf_op jit(solution)/shard_map/ppermute | solution.py:24
  83.5 0.4 collective-permute-start.15
  83.9 0.0 collective-permute-done.14.refs_0_
  83.9 3.3 %collective-permute-start.16 = (f32[3,8,512]{2,1,0:T(8,128)S(1)}, f32[3,8,512]{2,1,0:T(8,128)S(1)}, u32[]{:S(2)}, u32[]{:S(2)}) collective-permute-start(f32[3,8,512]{2,1,0:T(8,128)S(1)} %get-tuple-element.92), channel_id=1, source_target_pairs={{0,3},{1,0},{2,1},{3,2},{4,7},{5,4},{6,5},{7,6},{8,11},{9,8},{10,9... | collective-permute-start | bytes 147464 | tf_op jit(solution)/shard_map/ppermute | solution.py:24
  87.3 1.1 %smooth_y.2 = (f32[8,256,512]{2,1,0:T(8,128)}, f32[8,256,512]{2,1,0:T(8,128)}) custom-call(f32[3,64,512]{2,1,0:T(8,128)S(1)} %collective-permute-done.12.before_ref, f32[3,256,512]{2,1,0:T(8,128)S(1)} %complete.1.whole_ref, f32[3,64,512]{2,1,0:T(8,128)S(1)} %collective-permute-done.13.after_ref, f32[8,256,512]{2,1,0:T(8,128)S(1)} %copy-done), custom_call_target="tpu_custom_call" | custom-call | flops 4718592 | bytes 2359296 | tf_op jit(solution)/shard_map/smooth_y/pallas_call | solution.py:387
  88.4 1.4 %smooth_y.3 = (f32[8,256,512]{2,1,0:T(8,128)}, f32[8,256,512]{2,1,0:T(8,128)}) custom-call(f32[3,64,512]{2,1,0:T(8,128)S(1)} %collective-permute-done.12.before_ref, f32[3,256,512]{2,1,0:T(8,128)S(1)} %complete.1.whole_ref, f32[3,64,512]{2,1,0:T(8,128)S(1)} %collective-permute-done.13.after_ref, ...), custom_call_target="tpu_custom_call", output_to_operand_aliasing={{0}: (4, {}), {1}: (5, {})} | custom-call | flops 9437184 | bytes 4718592 | tf_op jit(solution)/shard_map/smooth_y/pallas_call | solution.py:387
  89.8 0.0 collective-permute-done.15.refs_1_
  89.8 0.0 collective-permute-done.16.refs_2_
  89.8 2.1 %finish_short.1 = (f32[8,256,512]{2,1,0:T(8,128)}, f32[8,256,512]{2,1,0:T(8,128)}) custom-call(f32[3,256,512]{2,1,0:T(8,128)S(1)} %get-tuple-element.83.whole_ref, f32[3,8,512]{2,1,0:T(8,128)S(1)} %collective-permute-done.14.refs_0_, f32[3,8,512]{2,1,0:T(8,128)S(1)} %collective-permute-done.15.refs_1_, ...), custom_call_target="tpu_custom_call", output_to_operand_aliasing={{0}: (5, {}), {1}: (6, {})} | custom-call | flops 12877824 | bytes 6438912 | tf_op jit(solution)/shard_map/finish_short/pallas_call | solution.py:387
  92.0 0.0 collective-permute-done.19.refs_1_
  92.0 1.3 %finish.2 = (f32[16,128,512]{2,1,0:T(8,128)}, f32[16,128,512]{2,1,0:T(8,128)}) custom-call(f32[2,120,512]{2,1,0:T(8,128)S(1)} %get-tuple-element.102.refs_0_, f32[2,120,512]{2,1,0:T(8,128)S(1)} %collective-permute-done.19.refs_1_, f32[16,128,512]{2,1,0:T(8,128)S(1)} %bitcast.7, ...), custom_call_target="tpu_custom_call", output_to_operand_aliasing={{0}: (3, {}), {1}: (4, {})} | custom-call | flops 5111808 | bytes 2555904 | tf_op jit(solution)/shard_map/finish/pallas_call | solution.py:387
  93.2 0.0 collective-permute-done.20.refs_1_
  93.2 1.0 %finish.3 = (f32[16,128,512]{2,1,0:T(8,128)}, f32[16,128,512]{2,1,0:T(8,128)}) custom-call(f32[1,120,512]{2,1,0:T(8,128)S(1)} %get-tuple-element.109.refs_0_, f32[1,120,512]{2,1,0:T(8,128)S(1)} %collective-permute-done.20.refs_1_, f32[16,128,512]{2,1,0:T(8,128)S(1)} %bitcast.8, ...), custom_call_target="tpu_custom_call", output_to_operand_aliasing={{0}: (3, {}), {1}: (4, {})} | custom-call | flops 2555904 | bytes 1277952 | tf_op jit(solution)/shard_map/finish/pallas_call | solution.py:387
  94.3 0.0 collective-permute-done.21.refs_1_
  94.3 1.0 %finish_last.1 = (f32[16,128,512]{2,1,0:T(8,128)}, f32[16,128,512]{2,1,0:T(8,128)}) custom-call(f32[1,120,512]{2,1,0:T(8,128)S(1)} %get-tuple-element.116.refs_0_, f32[1,120,512]{2,1,0:T(8,128)S(1)} %collective-permute-done.21.refs_1_, f32[16,128,512]{2,1,0:T(8,128)S(1)} %bitcast.9, ...), custom_call_target="tpu_custom_call", output_to_operand_aliasing={{0}: (3, {}), {1}: (4, {})} | custom-call | tf_op jit(solution)/shard_map/finish_last/pallas_call | solution.py:387
  (3 shorter events, 0.1 us)
Async XLA Ops:
  1.9 14.7 %collective-permute-start = (f32[2,120,512]{2,1,0:T(8,128)S(1)}, f32[2,120,512]{2,1,0:T(8,128)S(1)}, u32[]{:S(2)}, u32[]{:S(2)}) collective-permute-start(f32[2,120,512]{2,1,0:T(8,128)S(1)} %pair_x.1.refs_0_), channel_id=1, source_target_pairs={{0,16},{4,20},{8,24},{12,28},{16,0},{20,4},{24,8},{28,12},{1,17},{... | collective-permute-start | bytes 1474568 | tf_op jit(solution)/shard_map/ppermute | solution.py:24
  5.9 6.2 %collective-permute-start.5 = (f32[2,32,512]{2,1,0:T(8,128)S(1)}, f32[2,32,512]{2,1,0:T(8,128)S(1)}, u32[]{:S(2)}, u32[]{:S(2)}) collective-permute-start(f32[2,32,512]{2,1,0:T(8,128)S(1)} %slice.31), channel_id=1, source_target_pairs={{0,3},{1,0},{2,1},{3,2},{4,7},{5,4},{6,5},{7,6},{8,11},{9,8},{10,9... | collective-permute-start | bytes 393224 | tf_op jit(solution)/shard_map/ppermute | solution.py:24
  14.8 26.0 %collective-permute-start.6 = (f32[233,8,128]{2,1,0:T(8,128)S(1)}, f32[233,8,128]{2,1,0:T(8,128)S(1)}, u32[]{:S(2)}, u32[]{:S(2)}) collective-permute-start(f32[233,8,128]{2,1,0:T(8,128)S(1)} %smooth_yx_short.4.refs_0_), channel_id=1, source_target_pairs={{0,16},{4,20},{8,24},{12,28},{16,0},{20,4},{24,8},{28,12},{1,17},{... | collective-permute-start | bytes 2863112 | tf_op jit(solution)/shard_map/ppermute | solution.py:24
  17.7 11.1 %collective-permute-start.1 = (f32[2,64,512]{2,1,0:T(8,128)S(1)}, f32[2,64,512]{2,1,0:T(8,128)S(1)}, u32[]{:S(2)}, u32[]{:S(2)}) collective-permute-start(f32[2,64,512]{2,1,0:T(8,128)S(1)} %get-tuple-element.127), channel_id=1, source_target_pairs={{0,1},{1,2},{2,3},{3,0},{4,5},{5,6},{6,7},{7,4},{8,9},{9,10},{10,1... | collective-permute-start | bytes 786440 | tf_op jit(solution)/shard_map/ppermute | solution.py:24
  20.2 11.4 %collective-permute-start.2 = (f32[2,64,512]{2,1,0:T(8,128)S(1)}, f32[2,64,512]{2,1,0:T(8,128)S(1)}, u32[]{:S(2)}, u32[]{:S(2)}) collective-permute-start(f32[2,64,512]{2,1,0:T(8,128)S(1)} %get-tuple-element.126), channel_id=1, source_target_pairs={{0,3},{1,0},{2,1},{3,2},{4,7},{5,4},{6,5},{7,6},{8,11},{9,8},{10,9... | collective-permute-start | bytes 786440 | tf_op jit(solution)/shard_map/ppermute | solution.py:24
  34.3 41.2 %collective-permute-start.8 = (f32[233,8,128]{2,1,0:T(8,128)S(1)}, f32[233,8,128]{2,1,0:T(8,128)S(1)}, u32[]{:S(2)}, u32[]{:S(2)}) collective-permute-start(f32[233,8,128]{2,1,0:T(8,128)S(1)} %smooth_yx_short.3.refs_0_), channel_id=1, source_target_pairs={{0,16},{4,20},{8,24},{12,28},{16,0},{20,4},{24,8},{28,12},{1,17},{... | collective-permute-start | bytes 2863112 | tf_op jit(solution)/shard_map/ppermute | solution.py:24
  36.9 7.9 %collective-permute-start.3 = (f32[1,64,512]{2,1,0:T(8,128)S(1)}, f32[1,64,512]{2,1,0:T(8,128)S(1)}, u32[]{:S(2)}, u32[]{:S(2)}) collective-permute-start(f32[1,64,512]{2,1,0:T(8,128)S(1)} %get-tuple-element.125), channel_id=1, source_target_pairs={{0,1},{1,2},{2,3},{3,0},{4,5},{5,6},{6,7},{7,4},{8,9},{9,10},{10,1... | collective-permute-start | bytes 393224 | tf_op jit(solution)/shard_map/ppermute | solution.py:24
  38.1 7.0 %collective-permute-start.4 = (f32[1,64,512]{2,1,0:T(8,128)S(1)}, f32[1,64,512]{2,1,0:T(8,128)S(1)}, u32[]{:S(2)}, u32[]{:S(2)}) collective-permute-start(f32[1,64,512]{2,1,0:T(8,128)S(1)} %get-tuple-element.124), channel_id=1, source_target_pairs={{0,3},{1,0},{2,1},{3,2},{4,7},{5,4},{6,5},{7,6},{8,11},{9,8},{10,9... | collective-permute-start | bytes 393224 | tf_op jit(solution)/shard_map/ppermute | solution.py:24
  45.1 8.5 %collective-permute-start.9 = (f32[2,8,512]{2,1,0:T(8,128)S(1)}, f32[2,8,512]{2,1,0:T(8,128)S(1)}, u32[]{:S(2)}, u32[]{:S(2)}) collective-permute-start(f32[2,8,512]{2,1,0:T(8,128)S(1)} %get-tuple-element.80), channel_id=1, source_target_pairs={{0,1},{1,2},{2,3},{3,0},{4,5},{5,6},{6,7},{7,4},{8,9},{9,10},{10,1... | collective-permute-start | bytes 98312 | tf_op jit(solution)/shard_map/ppermute | solution.py:24
  45.4 11.1 %collective-permute-start.10 = (f32[2,8,512]{2,1,0:T(8,128)S(1)}, f32[2,8,512]{2,1,0:T(8,128)S(1)}, u32[]{:S(2)}, u32[]{:S(2)}) collective-permute-start(f32[2,8,512]{2,1,0:T(8,128)S(1)} %get-tuple-element.81), channel_id=1, source_target_pairs={{0,2},{1,3},{2,0},{3,1},{4,6},{5,7},{6,4},{7,5},{8,10},{9,11},{10,... | collective-permute-start | bytes 98312 | tf_op jit(solution)/shard_map/ppermute | solution.py:24
  48.5 8.4 %collective-permute-start.11 = (f32[2,8,512]{2,1,0:T(8,128)S(1)}, f32[2,8,512]{2,1,0:T(8,128)S(1)}, u32[]{:S(2)}, u32[]{:S(2)}) collective-permute-start(f32[2,8,512]{2,1,0:T(8,128)S(1)} %get-tuple-element.82), channel_id=1, source_target_pairs={{0,3},{1,0},{2,1},{3,2},{4,7},{5,4},{6,5},{7,6},{8,11},{9,8},{10,9... | collective-permute-start | bytes 98312 | tf_op jit(solution)/shard_map/ppermute | solution.py:24
  52.6 11.2 %collective-permute-start.17 = (f32[2,64,512]{2,1,0:T(8,128)S(1)}, f32[2,64,512]{2,1,0:T(8,128)S(1)}, u32[]{:S(2)}, u32[]{:S(2)}) collective-permute-start(f32[2,64,512]{2,1,0:T(8,128)S(1)} %get-tuple-element.123), channel_id=1, source_target_pairs={{0,1},{1,2},{2,3},{3,0},{4,5},{5,6},{6,7},{7,4},{8,9},{9,10},{10,1... | collective-permute-start | bytes 786440 | tf_op jit(solution)/shard_map/ppermute | solution.py:24
  53.6 13.9 %collective-permute-start.18 = (f32[2,64,512]{2,1,0:T(8,128)S(1)}, f32[2,64,512]{2,1,0:T(8,128)S(1)}, u32[]{:S(2)}, u32[]{:S(2)}) collective-permute-start(f32[2,64,512]{2,1,0:T(8,128)S(1)} %get-tuple-element.122), channel_id=1, source_target_pairs={{0,3},{1,0},{2,1},{3,2},{4,7},{5,4},{6,5},{7,6},{8,11},{9,8},{10,9... | collective-permute-start | bytes 786440 | tf_op jit(solution)/shard_map/ppermute | solution.py:24
  56.5 17.4 %collective-permute-start.7 = (f32[117,8,128]{2,1,0:T(8,128)S(1)}, f32[117,8,128]{2,1,0:T(8,128)S(1)}, u32[]{:S(2)}, u32[]{:S(2)}) collective-permute-start(f32[117,8,128]{2,1,0:T(8,128)S(1)} %smooth_yx_short.5.refs_0_), channel_id=1, source_target_pairs={{0,16},{4,20},{8,24},{12,28},{16,0},{20,4},{24,8},{28,12},{1,17},{... | collective-permute-start | bytes 1437704 | tf_op jit(solution)/shard_map/ppermute | solution.py:24
  57.1 30.2 %copy-start = (f32[8,256,512]{2,1,0:T(8,128)S(1)}, f32[8,256,512]{2,1,0:T(8,128)}, u32[]{:S(2)}) copy-start(f32[8,256,512]{2,1,0:T(8,128)} %c_ref.5) | copy-start | bytes 12582916
  57.1 19.9 %collective-permute-start.12 = (f32[3,64,512]{2,1,0:T(8,128)S(1)}, f32[3,64,512]{2,1,0:T(8,128)S(1)}, u32[]{:S(2)}, u32[]{:S(2)}) collective-permute-start(f32[3,64,512]{2,1,0:T(8,128)S(1)} %get-tuple-element.129), channel_id=1, source_target_pairs={{0,1},{1,2},{2,3},{3,0},{4,5},{5,6},{6,7},{7,4},{8,9},{9,10},{10,1... | collective-permute-start | bytes 1179656 | tf_op jit(solution)/shard_map/ppermute | solution.py:24
  70.7 21.2 %collective-permute-start.19 = (f32[2,120,512]{2,1,0:T(8,128)S(1)}, f32[2,120,512]{2,1,0:T(8,128)S(1)}, u32[]{:S(2)}, u32[]{:S(2)}) collective-permute-start(f32[2,120,512]{2,1,0:T(8,128)S(1)} %get-tuple-element.102.refs_0_), channel_id=1, source_target_pairs={{0,16},{4,20},{8,24},{12,28},{16,0},{20,4},{24,8},{28,12},{1,17},{... | collective-permute-start | bytes 1474568 | tf_op jit(solution)/shard_map/ppermute | solution.py:24
  70.8 12.7 %collective-permute-start.13 = (f32[3,64,512]{2,1,0:T(8,128)S(1)}, f32[3,64,512]{2,1,0:T(8,128)S(1)}, u32[]{:S(2)}, u32[]{:S(2)}) collective-permute-start(f32[3,64,512]{2,1,0:T(8,128)S(1)} %get-tuple-element.128), channel_id=1, source_target_pairs={{0,3},{1,0},{2,1},{3,2},{4,7},{5,4},{6,5},{7,6},{8,11},{9,8},{10,9... | collective-permute-start | bytes 1179656 | tf_op jit(solution)/shard_map/ppermute | solution.py:24
  73.9 19.3 %collective-permute-start.20 = (f32[1,120,512]{2,1,0:T(8,128)S(1)}, f32[1,120,512]{2,1,0:T(8,128)S(1)}, u32[]{:S(2)}, u32[]{:S(2)}) collective-permute-start(f32[1,120,512]{2,1,0:T(8,128)S(1)} %get-tuple-element.109.refs_0_), channel_id=1, source_target_pairs={{0,16},{4,20},{8,24},{12,28},{16,0},{20,4},{24,8},{28,12},{1,17},{... | collective-permute-start | bytes 737288 | tf_op jit(solution)/shard_map/ppermute | solution.py:24
  75.6 18.7 %collective-permute-start.21 = (f32[1,120,512]{2,1,0:T(8,128)S(1)}, f32[1,120,512]{2,1,0:T(8,128)S(1)}, u32[]{:S(2)}, u32[]{:S(2)}) collective-permute-start(f32[1,120,512]{2,1,0:T(8,128)S(1)} %get-tuple-element.116.refs_0_), channel_id=1, source_target_pairs={{0,16},{4,20},{8,24},{12,28},{16,0},{20,4},{24,8},{28,12},{1,17},{... | collective-permute-start | bytes 737288 | tf_op jit(solution)/shard_map/ppermute | solution.py:24
  77.0 7.0 %collective-permute-start.14 = (f32[3,8,512]{2,1,0:T(8,128)S(1)}, f32[3,8,512]{2,1,0:T(8,128)S(1)}, u32[]{:S(2)}, u32[]{:S(2)}) collective-permute-start(f32[3,8,512]{2,1,0:T(8,128)S(1)} %get-tuple-element.90), channel_id=1, source_target_pairs={{0,1},{1,2},{2,3},{3,0},{4,5},{5,6},{6,7},{7,4},{8,9},{9,10},{10,1... | collective-permute-start | bytes 147464 | tf_op jit(solution)/shard_map/ppermute | solution.py:24
  83.5 6.3 %collective-permute-start.15 = (f32[3,8,512]{2,1,0:T(8,128)S(1)}, f32[3,8,512]{2,1,0:T(8,128)S(1)}, u32[]{:S(2)}, u32[]{:S(2)}) collective-permute-start(f32[3,8,512]{2,1,0:T(8,128)S(1)} %get-tuple-element.91), channel_id=1, source_target_pairs={{0,2},{1,3},{2,0},{3,1},{4,6},{5,7},{6,4},{7,5},{8,10},{9,11},{10,... | collective-permute-start | bytes 147464 | tf_op jit(solution)/shard_map/ppermute | solution.py:24
  83.9 5.9 %collective-permute-start.16 = (f32[3,8,512]{2,1,0:T(8,128)S(1)}, f32[3,8,512]{2,1,0:T(8,128)S(1)}, u32[]{:S(2)}, u32[]{:S(2)}) collective-permute-start(f32[3,8,512]{2,1,0:T(8,128)S(1)} %get-tuple-element.92), channel_id=1, source_target_pairs={{0,3},{1,0},{2,1},{3,2},{4,7},{5,4},{6,5},{7,6},{8,11},{9,8},{10,9... | collective-permute-start | bytes 147464 | tf_op jit(solution)/shard_map/ppermute | solution.py:24
